TPU v7x, 32 devices: a whole 2x2x4 slice. The times are simulated.
32 devices in a mesh: grp: 4 (over y, core), own: 8 (over z, x).
Axes of the slice: x: 2, y: 2, z: 4, core: 2. Of those that a mesh axis runs over, the one named last changes fastest.
Arguments:
- fields: bfloat16 [192, 256, 128], P(None, 'grp'), may hold values from -6 to 6
- labels: int32 [192], replicated, may hold values 0 or 1
- pair_first: int32 [4, 8, 16], P('grp', 'own'), may hold values from 0 to 255, as said below
- pair_second: int32 [4, 8, 16], P(None, 'own'), may hold values from 0 to 255, as said below
- pair_count: int32 [4, 8], P('grp', 'own'), may hold values from 4 to 16, as said below
- pair_mats: float32 [4, 8, 16, 128, 128], P('grp', 'own'), may hold values from -6 to 6
Outputs:
- logits: float32 [192], replicated
- field_grad: float32 [192, 256, 128], P('own', 'grp')
- new_mats: float32 [4, 8, 16, 128, 128], P('grp', 'own')
Inputs may be any that keep to these rules, and one draw needn't show every extreme that they name: pair_first[g, o, s] lies in the block of fields g * 64 to (g + 1) * 64 - 1. `pair_second`: on every device (g, o), each block of 64 fields holds the second field of exactly 4 of the 16 slots; the second field is never the first. `pair_count`: slots at and beyond the count hold no pair; one device has all 16 slots live.
All inputs are finite; a program needn't handle non-finite values.
Results may differ from a plain program's by a relative error of at most 0.0003.
Values may be sent and summed in bfloat16 or wider, within the bound.
A program may use at most 64 MiB of HBM per device.

v0:
```python
import math

import jax
import jax.numpy as jnp
from jax import lax
from jax.sharding import PartitionSpec as P

STEPS = 2


logit_gain = 1.5
step_size = 1000.0
highest = lax.Precision.HIGHEST


def logit_errors(partial_value, targets, logit_scale):
    total_sum = lax.psum(partial_value, ("grp", "own"))
    logits = logit_scale * total_sum
    errors = jax.nn.sigmoid(logits) - targets
    return (logits, errors)


def on_device(fields, labels, pair_first, pair_second, pair_count, pair_mats):
    groups = lax.axis_size("grp")
    owners = lax.axis_size("own")
    my_group = lax.axis_index("grp")
    samples, per_block, feature = fields.shape
    slot_count = pair_first.shape[2]
    capacity = slot_count // groups
    second_table = pair_second[:, 0, :]
    block_ids = second_table // per_block
    offsets = second_table % per_block
    member = (block_ids[:, :, None] == jnp.arange(groups, dtype=jnp.int32)[None, None, :]).astype(
        jnp.int32
    )
    slot_ranks = jnp.sum((jnp.cumsum(member, axis=1) - 1) * member, axis=2)
    places = block_ids * capacity + slot_ranks
    chosen = (block_ids[:, :, None] == my_group) & (
        slot_ranks[:, :, None] == jnp.arange(capacity, dtype=jnp.int32)[None, None, :]
    )
    served = jnp.sum(jnp.where(chosen, offsets[:, :, None], 0), axis=1).reshape(-1)
    outgoing = jnp.take(fields, served, axis=1)
    incoming = lax.all_to_all(outgoing, "grp", split_axis=1, concat_axis=1, tiled=True)
    my_places = lax.dynamic_index_in_dim(places, my_group, 0, keepdims=False)
    second_vec = jnp.take(incoming, my_places, axis=1).astype(jnp.float32)
    first_local = pair_first[0, 0] - my_group * per_block
    first_vec = jnp.take(fields, first_local, axis=1).astype(jnp.float32)
    live_mask = (jnp.arange(slot_count, dtype=jnp.int32) < pair_count[0, 0]).astype(jnp.float32)
    matrices = pair_mats[0, 0]
    targets = labels.astype(jnp.float32)
    logit_scale = logit_gain / math.sqrt(groups * owners * slot_count)
    root_width = math.sqrt(feature)
    logits = jnp.zeros((samples,), jnp.float32)
    grad_first = jnp.zeros(first_vec.shape, jnp.float32)
    grad_second = jnp.zeros(first_vec.shape, jnp.float32)
    for step_index in range(STEPS):
        mixed = jnp.einsum("bsk,skl->bsl", first_vec, matrices, precision=highest)
        partial_value = jnp.sum(
            jnp.sum(mixed * second_vec, axis=2) / feature * live_mask[None, :], axis=1
        )
        logits, errors = logit_errors(partial_value, targets, logit_scale)
        if step_index == STEPS - 1:
            grad_first = (
                errors[:, None, None]
                * jnp.einsum("skl,bsl->bsk", matrices, second_vec, precision=highest)
                / root_width
                * live_mask[None, :, None]
            )
            grad_second = errors[:, None, None] * mixed / root_width * live_mask[None, :, None]
        gradient = jnp.einsum(
            "bsk,bsl->skl", first_vec * errors[:, None, None], second_vec, precision=highest
        )
        matrices = (
            matrices
            - step_size * logit_scale / (samples * feature) * live_mask[:, None, None] * gradient
        )
    slot_iota = jnp.arange(slot_count, dtype=jnp.int32)
    slot_of = jnp.sum(
        jnp.where(my_places[None, :] == slot_iota[:, None], slot_iota[None, :], 0), axis=1
    )
    returned = lax.all_to_all(
        jnp.take(grad_second, slot_of, axis=1), "grp", split_axis=1, concat_axis=1, tiled=True
    )
    block_iota = jnp.arange(per_block, dtype=jnp.int32)
    pick_second = (served[:, None] == block_iota[None, :]).astype(jnp.float32)
    pick_first = (first_local[:, None] == block_iota[None, :]).astype(jnp.float32)
    dense_grad = jnp.einsum("bsk,sf->bfk", grad_first, pick_first, precision=highest)
    dense_grad = dense_grad + jnp.einsum("bpk,pf->bfk", returned, pick_second, precision=highest)
    field_grad = lax.psum_scatter(dense_grad, "own", scatter_dimension=0, tiled=True)
    return (logits, field_grad, matrices[None, None])


def solution(mesh):
    in_specs = (
        P(None, "grp", None),
        P(),
        P("grp", "own", None),
        P(None, "own", None),
        P("grp", "own"),
        P("grp", "own", None, None, None),
    )
    out_specs = (P(), P("own", "grp", None), P("grp", "own", None, None, None))
    return jax.shard_map(
        on_device, mesh=mesh, in_specs=in_specs, out_specs=out_specs, check_vma=False
    )
```

profile of v0, /device:TPU:0, one launch (start us, length us, event | category | flops | bytes accessed | tf_op | source)
XLA Modules:
  0.0 294.1 jit_solution(13514963387786940270)
XLA Ops:
  7.2 0.8 add_select_fusion
  8.0 0.8 broadcast_compare_fusion
  9.4 4.2 %gather_fusion.3 = bf16[16,192,128]{2,0,1:T(8,128)(2,1)} fusion(bf16[192,64,128]{2,1,0:T(8,128)(2,1)S(1)} %copy-done, s32[1024]{0:T(1024)S(1)} %pad_clamp_fusion.2), kind=kCustom, calls=%fused_computation.1.clone | custom fusion | bytes 1572928 | tf_op jit(solution)/shard_map/jit(_take)/gather | solution.py:42
  13.6 1.3 select_bitcast_fusion.1
  14.9 1.1 copy.18
  16.0 4.2 %all-to-all-start = ((bf16[192,16,128]{2,0,1:T(8,128)(2,1)}), bf16[192,16,128]{2,0,1:T(8,128)(2,1)}, u32[]{:S(2)}, u32[]{:S(2)}) async-start(bf16[192,16,128]{2,0,1:T(8,128)(2,1)} %copy.18), calls=%async_computation | async-start | bytes 1572864 | tf_op jit(solution)/shard_map/all_to_all | solution.py:43
  21.1 4.2 %gather_fusion.2 = bf16[16,192,128]{2,0,1:T(8,128)(2,1)} fusion(bf16[192,64,128]{2,1,0:T(8,128)(2,1)S(1)} %copy-done, s32[1024]{0:T(1024)S(1)} %pad_clamp_fusion.3), kind=kCustom, calls=%fused_computation.clone | custom fusion | bytes 1572928 | tf_op jit(solution)/shard_map/jit(_take)/gather | solution.py:47
  25.3 7.2 %all-to-all-done = bf16[192,16,128]{2,0,1:T(8,128)(2,1)} async-done(((bf16[192,16,128]{2,0,1:T(8,128)(2,1)}), bf16[192,16,128]{2,0,1:T(8,128)(2,1)}, u32[]{:S(2)}, u32[]{:S(2)}) %all-to-all-start) | async-done | bytes 786464 | tf_op jit(solution)/shard_map/all_to_all | solution.py:43
  32.5 2.7 gather_fusion
  35.2 3.2 %fusion.2 = f32[192,16]{0,1:T(8,128)S(1)} fusion(f32[1,1,16,128,128]{4,3,2,1,0:T(8,128)} %param.13, bf16[16,192,128]{2,0,1:T(8,128)(2,1)} %gather_fusion.2, pred[16]{0:T(512)(128)(4,1)S(1)} %get-tuple-element.10, bf16[16,192,128]{2,1,0:T(8,128)(2,1)} %gather_fusion, pred[16]{0:T(512)(128)(4,1)S(1)} %get-tuple-element.14), kind=kOutput, calls=%fused_computation.11 | convolution fusion | flops 605942784 | bytes 2633760 | tf_op jit(solution)/shard_map/bsk,skl->bsl/dot_general | solution.py:57
  38.4 40.6 %psum.14 = f32[192]{0:T(256)S(1)} all-reduce(f32[192]{0:T(256)S(1)} %multiply_reduce_fusion.1), channel_id=1, replica_groups=mesh['grp'=4,'own'=8] {'grp','own'}, use_global_device_ids=true, to_apply=%region_5.7 | all-reduce | flops 192 | bytes 1536 | tf_op jit(solution)/shard_map/psum | solution.py:17
  79.0 3.9 %fusion.12 = f32[16,128,128]{2,1,0:T(8,128)S(1)} fusion(f32[1,1,16,128,128]{4,3,2,1,0:T(8,128)} %param.13, f32[192]{0:T(256)S(1)} %divide_subtract_fusion.1, f32[16]{0:T(128)S(1)} %fusion.37, bf16[16,192,128]{2,0,1:T(8,128)(2,1)} %gather_fusion.2, pred[16]{0:T(512)(128)(4,1)S(1)} %get-tuple-element.10, bf16[16,192,128]{2,1,0:T(8,128)(2,1)} %gather_fusion, ...), kind=kOutput, calls=%fused_computation.24 | convolution fusion | flops 606076928 | bytes 3670880 | tf_op jit(solution)/shard_map/bsk,bsl->skl/dot_general | solution.py:70
  82.9 2.3 fusion.3
  85.3 41.0 %psum.15 = f32[192]{0:T(256)S(1)} all-reduce(f32[192]{0:T(256)S(1)} %multiply_reduce_fusion), channel_id=1, replica_groups=mesh['grp'=4,'own'=8] {'grp','own'}, use_global_device_ids=true, to_apply=%region_8.10 | all-reduce | flops 192 | bytes 1536 | tf_op jit(solution)/shard_map/psum | solution.py:17
  126.9 2.8 fusion.4
  129.7 3.3 %gather_fusion.1 = f32[16,192,128]{2,1,0:T(8,128)} fusion(f32[192,16,128]{2,0,1:T(8,128)} %fusion.4, s32[1024]{0:T(1024)S(1)} %pad_clamp_fusion), kind=kCustom, calls=%fused_computation.3 | custom fusion | bytes 3145792 | tf_op jit(solution)/shard_map/jit(_take)/gather | solution.py:82
  133.0 2.8 select_bitcast_fusion
  135.8 4.4 %all-to-all-start.1 = ((f32[192,16,128]{2,0,1:T(8,128)}), f32[192,16,128]{2,0,1:T(8,128)}, u32[]{:S(2)}, u32[]{:S(2)}) async-start(f32[192,16,128]{2,0,1:T(8,128)} %select_bitcast_fusion), calls=%async_computation.1 | async-start | bytes 3145728 | tf_op jit(solution)/shard_map/all_to_all | solution.py:81
  140.5 2.7 multiply_bitcast_fusion
  143.1 5.6 %fusion.6 = f32[64,192,128]{2,0,1:T(8,128)} fusion(f32[192,16,128]{2,0,1:T(8,128)S(1)} %multiply_bitcast_fusion, s32[16]{0:T(128)S(1)} %get-tuple-element.11), kind=kOutput, calls=%fused_computation.16 | convolution fusion | flops 301990912 | bytes 7864384 | tf_op jit(solution)/shard_map/bsk,sf->bfk/dot_general | solution.py:87
  148.8 11.5 %all-to-all-done.1 = f32[192,16,128]{2,0,1:T(8,128)} async-done(((f32[192,16,128]{2,0,1:T(8,128)}), f32[192,16,128]{2,0,1:T(8,128)}, u32[]{:S(2)}, u32[]{:S(2)}) %all-to-all-start.1) | async-done | bytes 1572896 | tf_op jit(solution)/shard_map/all_to_all | solution.py:81
  160.3 9.1 %add_bitcast_fusion = f32[192,64,128]{2,1,0:T(8,128)} fusion(f32[64,192,128]{2,0,1:T(8,128)} %fusion.6, f32[192,16,128]{2,0,1:T(8,128)} %all-to-all-done.1, s32[16]{0:T(128)S(1)} %reshape.153), kind=kOutput, calls=%fused_computation.4 | convolution fusion | flops 303563776 | bytes 14155840 | tf_op jit(solution)/shard_map/bpk,pf->bfk/dot_general | solution.py:88
  169.4 4.7 %fusion.10 = f32[1,1,16,128,128]{4,3,2,1,0:T(8,128)} fusion(f32[16,128,128]{2,1,0:T(8,128)} %copy-done.2, f32[192]{0:T(256)S(1)} %get-tuple-element.4, f32[16]{0:T(128)S(1)} %fusion.37, bf16[16,192,128]{2,0,1:T(8,128)(2,1)} %gather_fusion.2, pred[16]{0:T(512)(128)(4,1)S(1)} %get-tuple-element.10, bf16[16,192,128]{2,1,0:T(8,128)(2,1)} %gather_fusion, ...), kind=kOutput, calls=%fused_computation.22 | convolution fusion | flops 606076928 | bytes 3670880 | tf_op jit(solution)/shard_map/bsk,bsl->skl/dot_general | solution.py:70
  174.1 113.2 %reduce-scatter.2.cloned.1.call-done = f32[24,64,128]{2,1,0:T(8,128)} async-done(((f32[192,64,128]{2,1,0:T(8,128)}), f32[24,64,128]{2,1,0:T(8,128)}) %reduce-scatter.2.cloned.1.call-update) | async-done | bytes 786448 | tf_op jit(solution)/shard_map/reduce_scatter | solution.py:89
  (39 shorter events, 1.8 us)
Async XLA Ops:
  7.2 2.2 copy-start
  14.9 6.0 %copy-start.5 = (s32[1,1,16]{2,1,0:T(1,128)S(1)}, s32[1,1,16]{2,1,0:T(1,128)}, u32[]{:S(2)}) copy-start(s32[1,1,16]{2,1,0:T(1,128)} %param.10) | copy-start | bytes 196
  16.0 16.5 %all-to-all-start = ((bf16[192,16,128]{2,0,1:T(8,128)(2,1)}), bf16[192,16,128]{2,0,1:T(8,128)(2,1)}, u32[]{:S(2)}, u32[]{:S(2)}) async-start(bf16[192,16,128]{2,0,1:T(8,128)(2,1)} %copy.18), calls=%async_computation | async-start | bytes 1572864 | tf_op jit(solution)/shard_map/all_to_all | solution.py:43
  35.2 43.8 %copy-start.4 = (s32[192]{0:T(256)S(1)}, s32[192]{0:T(256)}, u32[]{:S(2)}) copy-start(s32[192]{0:T(256)} %param.9) | copy-start | bytes 2308
  79.0 3.9 %copy-start.1 = (bf16[16,192,128]{2,1,0:T(8,128)(2,1)S(1)}, bf16[16,192,128]{2,1,0:T(8,128)(2,1)}, u32[]{:S(2)}) copy-start(bf16[16,192,128]{2,1,0:T(8,128)(2,1)} %gather_fusion) | copy-start | bytes 2359300
  79.0 3.9 %copy-start.3 = (bf16[16,192,128]{2,0,1:T(8,128)(2,1)S(1)}, bf16[16,192,128]{2,0,1:T(8,128)(2,1)}, u32[]{:S(2)}) copy-start(bf16[16,192,128]{2,0,1:T(8,128)(2,1)} %gather_fusion.2) | copy-start | bytes 2359300
  82.9 2.3 copy-start.2
  135.8 24.5 %all-to-all-start.1 = ((f32[192,16,128]{2,0,1:T(8,128)}), f32[192,16,128]{2,0,1:T(8,128)}, u32[]{:S(2)}, u32[]{:S(2)}) async-start(f32[192,16,128]{2,0,1:T(8,128)} %select_bitcast_fusion), calls=%async_computation.1 | async-start | bytes 3145728 | tf_op jit(solution)/shard_map/all_to_all | solution.py:81
  140.2 147.1 %reduce-scatter.2.cloned.1.call-start = ((), (), s32[]{:S(2)}) async-start(), calls=%async_computation.3 | async-start | bytes 7077888 | tf_op jit(solution)/shard_map/reduce_scatter | solution.py:89
Sparse Core Ops, SparseCore 0:
  169.5 117.7 reduce-scatter.1
where the time goes:
time: 295 us; the launch traced here: 294 us
  waiting for transfers between devices  132 us (45%)
  blocking collectives  81.6 us (28%)
  matrix products  31.4 us (11%)
  local copies, waits for them, and re-layouts  15.6 us (5%)
  between operations  14.9 us (5%)
  other arithmetic  9.97 us (3%)
  starting transfers between devices  8.87 us (3%)
    reduce_scatter x1, waiting for transfers between devices, on_device(): lax.psum_scatter(dense_grad, 'own', scatter_dimension=0, tiled=True)  113 us
    psum x2, blocking collectives, logit_errors(): total_sum = lax.psum(partial_value, ('grp', 'own'))  81.6 us
    all_to_all x1, waiting for transfers between devices, on_device(): lax.all_to_all(jnp.take(grad_second, slot_of, axis=1), 'grp', split_axis=...  11.5 us
    dot_general x1, matrix products, on_device(): jnp.einsum('bpk,pf->bfk', returned, pick_second, precision=highest)  9.06 us
    dot_general x2, matrix products, on_device(): jnp.einsum('bsk,bsl->skl', first_vec * errors[:, None, None], second_vec,...  8.58 us
    all_to_all x1, waiting for transfers between devices, on_device(): lax.all_to_all(outgoing, 'grp', split_axis=1, concat_axis=1, tiled=True)  7.17 us
  transfers between devices with their start and end apart: 3, of which 3 were waited for; matrix products, arithmetic and copies ran while one was open for 6% of the time, Pallas kernels for 0%

commit v1 on v0

--- a/solution.py
+++ b/solution.py
@@ -1,8 +1,11 @@
+import functools
 import math
 
 import jax
 import jax.numpy as jnp
 from jax import lax
+from jax.experimental import pallas as pl
+from jax.experimental.pallas import tpu as pltpu
 from jax.sharding import PartitionSpec as P
 
 STEPS = 2
@@ -90,6 +93,508 @@
     return (logits, field_grad, matrices[None, None])
 
 
+LANES = 128
+SUB = 8
+TOP = 32760.0
+MESH = pl.DeviceIdType.MESH
+NT = (((1,), (1,)), ((), ()))
+
+
+def two_parts(x):
+    high = x.astype(jnp.bfloat16)
+    low = (x - high.astype(jnp.float32)).astype(jnp.bfloat16)
+    return high, low
+
+
+def dot32(a, b):
+    return jnp.dot(a, b, preferred_element_type=jnp.float32)
+
+
+def step_kernel(
+    groups, owners,
+    slot_of, places, live_place,
+    fields, tcol, msg0, targets, mats,
+    logits_out, grad_out, mats_out,
+    first_vec, first_t, served_vec, second_vec, mats_mid, total,
+    msg1, got1, msg2, got2, term_a, term_b, send_a, send_b, got_a, got_b, err_col, acc,
+    sem_v, sem_m1, sem_m2, sem_a, sem_b,
+):
+    samples, per_block, feature = fields.shape
+    slots = mats.shape[0]
+    cap = slots // groups
+    chunk = samples // owners
+    devices = groups * owners
+    pairs = cap // 2
+    g, o = lax.axis_index("grp"), lax.axis_index("own")
+    me = g * owners + o
+    logit_scale = logit_gain / math.sqrt(devices * slots)
+    rate = step_size * logit_scale / (samples * feature)
+    inv_root = 1.0 / math.sqrt(feature)
+    extra = 2 * LANES - samples
+
+    barrier = pltpu.get_barrier_semaphore()
+
+    def greet(d, _):
+        peer = lax.rem(me + d, devices)
+        pl.semaphore_signal(
+            barrier, inc=1, device_id=(lax.div(peer, owners), lax.rem(peer, owners)), device_id_type=MESH
+        )
+        return 0
+
+    lax.fori_loop(1, devices, greet, 0)
+
+    def gather(lo, out):
+        wide = SUB * per_block
+        rows = slots * SUB
+        lanes = lax.broadcasted_iota(jnp.int32, (rows, wide), 1)
+        pick = jnp.where(lanes == tcol[lo : lo + rows, :], 1.0, 0.0).astype(jnp.bfloat16)
+
+        def part(i, _):
+            halves = []
+            for h in range(2):
+                block = fields[pl.ds(i * 16 + h * SUB, SUB)].reshape(wide, feature)
+                halves.append(dot32(pick, block).reshape(slots, SUB, feature))
+            out[:, pl.ds(pl.multiple_of(i * 16, 16), 16), :] = jnp.concatenate(halves, axis=1).astype(jnp.bfloat16)
+            return 0
+
+        lax.fori_loop(0, samples // 16, part, 0)
+
+    def vec_copy(j):
+        to = lax.rem(g + j, groups)
+        return pltpu.make_async_remote_copy(
+            src_ref=served_vec.at[pl.ds(to * cap, cap)],
+            dst_ref=second_vec.at[pl.ds(g * cap, cap)],
+            send_sem=sem_v.at[0, j],
+            recv_sem=sem_v.at[1, j],
+            device_id=(to, o),
+            device_id_type=MESH,
+        )
+
+    gather(slots * SUB, served_vec)
+    pl.semaphore_wait(barrier, devices - 1)
+    for j in range(1, groups):
+        vec_copy(j).start()
+    second_vec[pl.ds(g * cap, cap)] = served_vec[pl.ds(g * cap, cap)]
+    gather(0, first_vec)
+
+    def turn(p, _):
+        v = first_vec[p].astype(jnp.float32)
+        v = jnp.concatenate([v, jnp.zeros((extra, feature), jnp.float32)], axis=0)
+        first_t[p] = v.T.astype(jnp.bfloat16)
+        return 0
+
+    lax.fori_loop(0, slots, turn, 0)
+    total[...] = jnp.zeros_like(total)
+
+    def mix(p, mat):
+        v1 = first_vec[p]
+        high, low = two_parts(mat)
+        return dot32(jnp.concatenate([v1, v1], axis=1), jnp.concatenate([high, low], axis=0)), high, low
+
+    def first_pass(q):
+        sums = total[...]
+        for c in range(cap):
+            p = q * cap + c
+            mixed, _, _ = mix(p, mats[slot_of[p]])
+            sums = sums + (mixed * second_vec[p].astype(jnp.float32)) * live_place[p]
+        total[...] = sums
+
+    first_pass(g)
+    for j in range(1, groups):
+        vec_copy(j).wait_recv()
+        first_pass(lax.rem(g + groups - j, groups))
+
+    def partial_rows():
+        ones = jnp.ones((SUB, feature), jnp.float32)
+        tail = jnp.concatenate([total[LANES:samples], jnp.zeros((extra, feature), jnp.float32)], axis=0)
+        return [
+            lax.dot_general(ones, t, NT, precision=highest, preferred_element_type=jnp.float32)
+            for t in (total[0:LANES], tail)
+        ]
+
+    row_id = lax.broadcasted_iota(jnp.int32, (SUB, LANES), 0)
+    r0, r1 = partial_rows()
+    for q in range(groups):
+        msg1[q] = jnp.where(row_id == 0, r0, jnp.where(row_id == 1, r1, msg0[q]))
+
+    def tile_copy(src, dst, sems, d, pick_own):
+        peer = lax.rem(me + d, devices)
+        pg, po = lax.div(peer, owners), lax.rem(peer, owners)
+        return pltpu.make_async_remote_copy(
+            src_ref=src.at[po if pick_own else pg],
+            dst_ref=dst.at[me],
+            send_sem=sems.at[0, peer],
+            recv_sem=sems.at[1, me],
+            device_id=(pg, po),
+            device_id_type=MESH,
+        )
+
+    def tile_arrival(src, dst, sems, d):
+        peer = lax.rem(me + d, devices)
+        return pltpu.make_async_remote_copy(
+            src_ref=src.at[0],
+            dst_ref=dst.at[peer],
+            send_sem=sems.at[0, peer],
+            recv_sem=sems.at[1, peer],
+            device_id=(lax.div(peer, owners), lax.rem(peer, owners)),
+            device_id_type=MESH,
+        )
+
+    def send_tiles(src, dst, sems, pick_own):
+        def one(d, _):
+            tile_copy(src, dst, sems, d, pick_own).start()
+            return 0
+
+        lax.fori_loop(1, devices, one, 0)
+
+    def wait_tiles(src, dst, sems):
+        def one(d, _):
+            tile_arrival(src, dst, sems, d).wait_recv()
+            return 0
+
+        lax.fori_loop(1, devices, one, 0)
+
+    def errors_of(got, at):
+        sums = got[0]
+        for d in range(1, devices):
+            sums = sums + got[d]
+        sums = sums[at : at + 2] * (1.0 / feature)
+        logits = logit_scale * sums
+        return logits, jax.nn.sigmoid(logits) - targets[0:2]
+
+    def error_row(err):
+        return jnp.concatenate([err[0:1], err[1:2, 0 : samples - LANES]], axis=1)
+
+    def gradient(p, erow):
+        v = first_t[p][:, 0:samples].astype(jnp.float32) * erow
+        high, low = two_parts(v)
+        v2 = second_vec[p]
+        return dot32(high, v2) + dot32(low, v2)
+
+    send_tiles(msg1, got1, sem_m1, False)
+    got1[me] = msg1[g]
+    wait_tiles(msg1, got1, sem_m1)
+    _, err = errors_of(got1, 0)
+    erow = error_row(err)
+    total[...] = jnp.zeros_like(total)
+    msg2[...] = jnp.zeros_like(msg2)
+
+    def second_pass(j):
+        q = lax.rem(g + j, groups)
+        sums = total[...]
+        for c in range(cap):
+            p = q * cap + c
+            live = live_place[p]
+            mid = mats[slot_of[p]] - (rate * live) * gradient(p, erow)
+            mats_mid[p] = mid
+            mixed, high, low = mix(p, mid)
+            v2 = second_vec[p]
+            first = lax.dot_general(
+                jnp.concatenate([v2, v2], axis=1),
+                jnp.concatenate([high, low], axis=1),
+                NT,
+                preferred_element_type=jnp.float32,
+            )
+            sums = sums + (mixed * v2.astype(jnp.float32)) * live
+            factor = live * inv_root
+            term_a[c] = first * factor
+            term_b[c] = mixed * factor
+        total[...] = sums
+
+        def code(w, _):
+            rows = pl.ds(pl.multiple_of(w * chunk, SUB), chunk)
+            terms = [t[c, rows, :] for t in (term_a, term_b) for c in range(cap)]
+            big = functools.reduce(jnp.maximum, [jnp.abs(t) for t in terms])
+            big = jnp.maximum(jnp.max(big, axis=0, keepdims=True), 1e-30)
+            gain = TOP / big
+            whole = [jnp.floor(t * gain + 0.5).astype(jnp.int32) for t in terms]
+            for at, out in ((0, send_a), (cap, send_b)):
+                for k in range(pairs):
+                    a, b = whole[at + 2 * k], whole[at + 2 * k + 1]
+                    out[q, w, pl.ds(k * chunk, chunk), :] = (a & 0xFFFF) | (b << 16)
+            msg2[w, pl.ds(q, 1), :] = big * (1.0 / TOP)
+            return 0
+
+        lax.fori_loop(0, owners, code, 0)
+
+    def unit_a(j, k):
+        q, w = lax.rem(g + j, groups), lax.rem(o + k, owners)
+        return pltpu.make_async_remote_copy(
+            src_ref=send_a.at[q, w], dst_ref=got_a.at[o, q], send_sem=sem_a.at[0, q, w],
+            recv_sem=sem_a.at[1, q, o], device_id=(g, w), device_id_type=MESH,
+        )
+
+    def unit_b(j, k):
+        q, w = lax.rem(g + j, groups), lax.rem(o + k, owners)
+        return pltpu.make_async_remote_copy(
+            src_ref=send_b.at[q, w], dst_ref=got_b.at[g, o], send_sem=sem_b.at[0, q, w],
+            recv_sem=sem_b.at[1, g, o], device_id=(q, w), device_id_type=MESH,
+        )
+
+    def send_units(j):
+        def one(k, _):
+            unit_a(j, k).start()
+            unit_b(j, k).start()
+            return 0
+
+        lax.fori_loop(1, owners, one, 0)
+        q = lax.rem(g + j, groups)
+        got_a[o, q] = send_a[q, o]
+
+    second_pass(0)
+    got_b[g, o] = send_b[g, o]
+    send_units(0)
+
+    def middle(j, _):
+        second_pass(j)
+        send_units(j)
+        unit_b(j, 0).start()
+        return 0
+
+    lax.fori_loop(1, groups - 1, middle, 0)
+    second_pass(groups - 1)
+    r0, r1 = partial_rows()
+    for w in range(owners):
+        msg2[w] = jnp.where(row_id == groups, r0, jnp.where(row_id == groups + 1, r1, msg2[w]))
+    send_tiles(msg2, got2, sem_m2, True)
+    send_units(groups - 1)
+    unit_b(groups - 1, 0).start()
+    got2[me] = msg2[o]
+    wait_tiles(msg2, got2, sem_m2)
+    logits, err = errors_of(got2, groups)
+    logits_out[...] = jnp.concatenate([logits, jnp.zeros((SUB - 2, LANES), jnp.float32)], axis=0)
+    erow = error_row(err)
+    eye = lax.broadcasted_iota(jnp.int32, (LANES, LANES), 0) == lax.broadcasted_iota(jnp.int32, (LANES, LANES), 1)
+    for half in range(2):
+        column = jnp.sum(jnp.where(eye, err[half : half + 1], 0.0), axis=1, keepdims=True)
+        err_col[pl.ds(half * LANES, LANES), :] = jnp.broadcast_to(column, (LANES, LANES))
+
+    def last_update(s, _):
+        p = places[s]
+        mats_out[s] = mats_mid[p] - (rate * live_place[p]) * gradient(p, erow)
+        return 0
+
+    lax.fori_loop(0, slots, last_update, 0)
+
+    col = err_col[pl.ds(pl.multiple_of(o * chunk, SUB), chunk), :]
+    parts = chunk // SUB
+    field_rows = lax.broadcasted_iota(jnp.int32, (SUB * per_block, LANES), 0)
+
+    def decode(word_of, scale):
+        out = []
+        factor = col * scale
+        for k in range(pairs):
+            w = word_of(k)
+            out.append(((w << 16) >> 16).astype(jnp.float32) * factor)
+            out.append((w >> 16).astype(jnp.float32) * factor)
+        return out
+
+    def place_terms(terms, spots, fresh=False):
+        spots = (spots + 0.5).astype(jnp.int32)
+        pick = jnp.where(field_rows == spots, 1.0, 0.0).astype(jnp.bfloat16)
+        x = jnp.concatenate(
+            [jnp.concatenate([t[i * SUB : (i + 1) * SUB] for t in terms], axis=0) for i in range(parts)], axis=1
+        )
+        high, low = two_parts(x)
+        out = dot32(jnp.concatenate([pick, pick], axis=1), jnp.concatenate([high, low], axis=0))
+        acc[...] = out if fresh else acc[...] + out
+
+    span = LANES // (cap * SUB)
+
+    acc[...] = jnp.zeros_like(acc)
+
+    def arrive_b(j, k):
+        @pl.when(j + k > 0)
+        def _():
+            q, w = lax.rem(g + groups - j, groups), lax.rem(o + owners - k, owners)
+            pltpu.make_async_remote_copy(
+                src_ref=send_b.at[q, w], dst_ref=got_b.at[q, w], send_sem=sem_b.at[0, q, w],
+                recv_sem=sem_b.at[1, q, w], device_id=(q, w), device_id_type=MESH,
+            ).wait_recv()
+
+    def from_seconds(j, _):
+        q = lax.rem(g + groups - j, groups)
+
+        def one(k, _):
+            arrive_b(j, k)
+            return 0
+
+        lax.fori_loop(0, owners, one, 0)
+
+        def half(h, _):
+            terms, spots = [], 0.0
+            for i in range(span):
+                w = h * span + i
+                src = q * owners + w
+                scale = got2[src, pl.ds(g, 1), :]
+                terms += decode(lambda k: got_b[q, w, pl.ds(k * chunk, chunk), :], scale)
+                spots = spots + got1[src][3:4]
+            place_terms(terms, spots)
+            return 0
+
+        lax.fori_loop(0, owners // span, half, 0)
+        return 0
+
+    lax.fori_loop(0, groups, from_seconds, 0)
+
+    def from_firsts(k, _):
+        w = lax.rem(o + owners - k, owners)
+        src = g * owners + w
+
+        @pl.when(k > 0)
+        def _():
+            for q in range(groups):
+                pltpu.make_async_remote_copy(
+                    src_ref=send_a.at[q, w], dst_ref=got_a.at[w, q], send_sem=sem_a.at[0, q, w],
+                    recv_sem=sem_a.at[1, q, w], device_id=(g, w), device_id_type=MESH,
+                ).wait_recv()
+
+        terms = []
+        for q in range(groups):
+            scale = got2[src][q : q + 1]
+            terms += decode(lambda m: got_a[w, q, pl.ds(m * chunk, chunk), :], scale)
+        place_terms(terms, got1[src][2:3])
+        return 0
+
+    lax.fori_loop(0, owners, from_firsts, 0)
+    for i in range(parts):
+        grad_out[i * SUB : (i + 1) * SUB] = acc[:, i * feature : (i + 1) * feature].reshape(SUB, per_block, feature)
+
+    for j in range(1, groups):
+        vec_copy(j).wait_send()
+
+    def drain_tiles(d, _):
+        tile_copy(msg1, got1, sem_m1, d, False).wait_send()
+        tile_copy(msg2, got2, sem_m2, d, True).wait_send()
+        return 0
+
+    lax.fori_loop(1, devices, drain_tiles, 0)
+
+    def drain_units(j, _):
+        def one(k, _):
+            unit_a(j, k).wait_send()
+            unit_b(j, k).wait_send()
+            return 0
+
+        lax.fori_loop(1, owners, one, 0)
+
+        @pl.when(j > 0)
+        def _():
+            unit_b(j, 0).wait_send()
+
+        return 0
+
+    lax.fori_loop(0, groups, drain_units, 0)
+
+
+def on_device_kernel(fields, labels, pair_first, pair_second, pair_count, pair_mats):
+    groups = lax.axis_size("grp")
+    owners = lax.axis_size("own")
+    g, o = lax.axis_index("grp"), lax.axis_index("own")
+    samples, per_block, feature = fields.shape
+    slots = pair_first.shape[2]
+    cap = slots // groups
+    chunk = samples // owners
+    devices = groups * owners
+    table = pair_second[:, 0, :]
+    block_ids = table // per_block
+    offsets = table % per_block
+    same = block_ids[:, :, None] == block_ids[:, None, :]
+    slot_iota = jnp.arange(slots, dtype=jnp.int32)
+    before = slot_iota[None, :] < slot_iota[:, None]
+    ranks = jnp.sum((same & before[None]).astype(jnp.int32), axis=2)
+    places_all = block_ids * cap + ranks
+    match = places_all[:, :, None] == slot_iota[None, None, :]
+    off_place = jnp.sum(jnp.where(match, offsets[:, :, None], 0), axis=1)
+    served = lax.dynamic_slice_in_dim(off_place, g * cap, cap, axis=1).reshape(-1)
+    places = lax.dynamic_index_in_dim(places_all, g, 0, keepdims=False)
+    mine = places[:, None] == slot_iota[None, :]
+    slot_of = jnp.sum(jnp.where(mine, slot_iota[:, None], 0), axis=0)
+    first_local = pair_first[0, 0] - g * per_block
+    first_place = jnp.sum(jnp.where(mine, first_local[:, None], 0), axis=0)
+    second_place = lax.dynamic_index_in_dim(off_place, g, 0, keepdims=False)
+    live_place = (slot_of < pair_count[0, 0]).astype(jnp.float32)
+    lift = jnp.arange(SUB, dtype=jnp.int32) * per_block
+    spots = lambda idx: (idx[:, None] + lift[None, :]).reshape(-1)
+    tcol = spots(jnp.concatenate([first_place, served]))[:, None]
+    span = LANES // (cap * SUB)
+    segments = jnp.tile(spots(second_place).reshape(groups, cap * SUB), (1, span))
+    lane_seg = jnp.arange(LANES, dtype=jnp.int32) // (cap * SUB)
+    segments = jnp.where(lane_seg[None, :] == o % span, segments, 0)
+    firsts = jnp.broadcast_to(spots(first_place)[None], (groups, LANES))
+    zero = jnp.zeros((groups, 2, LANES), jnp.int32)
+    msg0 = jnp.concatenate([zero, firsts[:, None], segments[:, None], zero, zero], axis=1).astype(jnp.float32)
+    targets = jnp.pad(labels.astype(jnp.float32), (0, SUB * LANES - samples)).reshape(SUB, LANES)
+    smem = pl.BlockSpec(memory_space=pltpu.SMEM)
+    vmem = pl.BlockSpec(memory_space=pltpu.VMEM)
+    rows = cap // 2 * chunk
+    f32, bf16, i32 = jnp.float32, jnp.bfloat16, jnp.int32
+    logits, grad, new_mats = pl.pallas_call(
+        functools.partial(step_kernel, groups, owners),
+        out_shape=(
+            jax.ShapeDtypeStruct((SUB, LANES), f32),
+            jax.ShapeDtypeStruct((chunk, per_block, feature), f32),
+            jax.ShapeDtypeStruct((slots, feature, feature), f32),
+        ),
+        in_specs=[smem] * 3 + [vmem] * 5,
+        out_specs=(vmem,) * 3,
+        scratch_shapes=[
+            pltpu.VMEM((slots, samples, feature), bf16),
+            pltpu.VMEM((slots, feature, 2 * LANES), bf16),
+            pltpu.VMEM((slots, samples, feature), bf16),
+            pltpu.VMEM((slots, samples, feature), bf16),
+            pltpu.VMEM((slots, feature, feature), f32),
+            pltpu.VMEM((samples, feature), f32),
+            pltpu.VMEM((groups, SUB, LANES), f32),
+            pltpu.VMEM((devices, SUB, LANES), f32),
+            pltpu.VMEM((owners, SUB, LANES), f32),
+            pltpu.VMEM((devices, SUB, LANES), f32),
+            pltpu.VMEM((cap, samples, feature), f32),
+            pltpu.VMEM((cap, samples, feature), f32),
+            pltpu.VMEM((groups, owners, rows, feature), i32),
+            pltpu.VMEM((groups, owners, rows, feature), i32),
+            pltpu.VMEM((owners, groups, rows, feature), i32),
+            pltpu.VMEM((groups, owners, rows, feature), i32),
+            pltpu.VMEM((2 * LANES, LANES), f32),
+            pltpu.VMEM((SUB * per_block, chunk // SUB * feature), f32),
+            pltpu.SemaphoreType.DMA((2, groups)),
+            pltpu.SemaphoreType.DMA((2, devices)),
+            pltpu.SemaphoreType.DMA((2, devices)),
+            pltpu.SemaphoreType.DMA((2, groups, owners)),
+            pltpu.SemaphoreType.DMA((2, groups, owners)),
+        ],
+        compiler_params=pltpu.CompilerParams(
+            collective_id=0, has_side_effects=True, vmem_limit_bytes=40 * 1024 * 1024
+        ),
+        cost_estimate=pl.CostEstimate(flops=4 * 10**9, bytes_accessed=8 * 10**6, transcendentals=400),
+    )(slot_of, places, live_place, fields, tcol, msg0, targets, pair_mats[0, 0])
+    return (logits.reshape(-1)[:samples], grad, new_mats[None, None])
+
+
+def fits(groups, owners, fields, pair_first):
+    samples, _, feature = fields.shape
+    slots = pair_first.shape[2]
+    cap = slots // groups
+    return (
+        feature == LANES
+        and slots * SUB == LANES
+        and slots % groups == 0
+        and cap % 2 == 0
+        and LANES < samples <= 2 * LANES
+        and samples % (SUB * owners) == 0
+        and samples % 16 == 0
+        and owners % (LANES // (cap * SUB)) == 0
+        and groups + 2 <= SUB
+    )
+
+
+def dispatch(groups, owners, fields, labels, pair_first, pair_second, pair_count, pair_mats):
+    args = (fields, labels, pair_first, pair_second, pair_count, pair_mats)
+    if fits(groups, owners, fields, pair_first):
+        return on_device_kernel(*args)
+    return on_device(*args)
+
+
 def solution(mesh):
     in_specs = (
         P(None, "grp", None),
@@ -100,6 +605,7 @@
         P("grp", "own", None, None, None),
     )
     out_specs = (P(), P("own", "grp", None), P("grp", "own", None, None, None))
+    per_device = functools.partial(dispatch, mesh.shape["grp"], mesh.shape["own"])
     return jax.shard_map(
-        on_device, mesh=mesh, in_specs=in_specs, out_specs=out_specs, check_vma=False
+        per_device, mesh=mesh, in_specs=in_specs, out_specs=out_specs, check_vma=False
     )

time: 295 us -> 83.7 us (0.28)
  waiting for transfers between devices: 132 us -> 0 us
  blocking collectives: 81.6 us -> 0 us
  Pallas kernels: 0 us -> 72.2 us
  matrix products: 31.4 us -> 0 us
  between operations: 14.9 us -> 1.38 us
  local copies, waits for them, and re-layouts: 15.6 us -> 6.42 us
  starting transfers between devices: 8.87 us -> 0 us
  other arithmetic: 9.97 us -> 3.47 us
    reduce_scatter x1 -> x0, waiting for transfers between devices: 113 us -> none  [on_device(): lax.psum_scatter(dense_grad, 'own', scatter_dimension=0, tiled=True)]
    psum x2 -> x0, blocking collectives: 81.6 us -> none  [logit_errors(): total_sum = lax.psum(partial_value, ('grp', 'own'))]
    pallas_call x0 -> x1, Pallas kernels: none -> 72.2 us  [on_device_kernel(): pl.pallas_call(functools.partial(step_kernel, groups, owners), out_shape=...]
    dot_general x7 -> x0, matrix products: 31.4 us -> none  [the longest x1 9.06 us: on_device(): jnp.einsum('bpk,pf->bfk', returned, pick_second, precision=highest)]
    all_to_all x2 -> x0, waiting for transfers between devices: 18.7 us -> none  [the longest x1 11.5 us: on_device(): lax.all_to_all(jnp.take(grad_second, slot_of, axis=1), 'grp', split_axis=...]
    gather x4 -> x0, local copies, waits for them, and re-layouts: 14.4 us -> none  [the longest x1 4.23 us: on_device(): first_vec = jnp.take(fields, first_local, axis=1).astype(jnp.float32)]
    all_to_all x2 -> x0, starting transfers between devices: 8.6 us -> none  [the longest x1 4.37 us: on_device(): lax.all_to_all(jnp.take(grad_second, slot_of, axis=1), 'grp', split_axis=...]
    unnamed x12 -> x6, local copies, waits for them, and re-layouts: 0.03 us -> 4.96 us
  transfers between devices with their start and end apart: 3 -> 0, of which waited for: 3 -> 0; matrix products, arithmetic and copies ran while one was open for 6% -> 0% of each run, Pallas kernels for 0% -> 0%
where the time goes in v1:
time: 83.7 us; the launch traced here: 83.4 us
  Pallas kernels  72.2 us (86%)
  local copies, waits for them, and re-layouts  6.42 us (8%)
  other arithmetic  3.47 us (4%)
  between operations  1.38 us (2%)
    pallas_call x1, Pallas kernels, on_device_kernel(): pl.pallas_call(functools.partial(step_kernel, groups, owners), out_shape=...  72.2 us
    unnamed x6, local copies, waits for them, and re-layouts  4.96 us

profile of v1, /device:TPU:0, one launch (start us, length us, event | category | flops | bytes accessed | tf_op | source)
XLA Modules:
  0.0 83.4 jit_solution(16269033134883148405)
XLA Ops:
  1.3 0.7 subtract_bitcast_fusion
  2.0 0.1 pad.8.clone
  2.1 0.7 convert_element_type.17
  2.7 0.1 add.130
  2.8 0.7 and_select_fusion
  3.6 0.7 add_select_fusion
  4.2 0.2 convert_reduce_fusion
  4.5 0.1 select_reduce_fusion
  4.6 0.1 constant_dynamic-slice_fusion.1
  4.7 0.1 reshape.212
  4.8 0.1 select_reduce_fusion.1
  4.9 0.1 pad_add_fusion
  5.0 0.1 add.126
  5.1 0.1 add.128
  5.2 0.1 tile.9
  5.4 0.1 add.124
  5.5 0.1 add_convert_fusion.msg0
  5.6 0.1 add.133.tcol
  5.7 1.9 %copy-done = bf16[192,64,128]{2,1,0:T(8,128)(2,1)S(1)} copy-done((bf16[192,64,128]{2,1,0:T(8,128)(2,1)S(1)}, bf16[192,64,128]{2,1,0:T(8,128)(2,1)}, u32[]{:S(2)}) %copy-start) | copy-done | bytes 3145752
  7.6 1.2 %copy-done.1 = f32[1,1,16,128,128]{4,3,2,1,0:T(8,128)S(1)} copy-done((f32[1,1,16,128,128]{4,3,2,1,0:T(8,128)S(1)}, f32[1,1,16,128,128]{4,3,2,1,0:T(8,128)}, u32[]{:S(2)}) %copy-start.1) | copy-done | bytes 1048600
  8.9 72.2 %shard_map.85 = (f32[8,128]{1,0:T(8,128)S(1)}, f32[24,64,128]{2,1,0:T(8,128)S(1)}, f32[16,128,128]{2,1,0:T(8,128)S(1)}) custom-call(s32[16]{0:T(128)S(1)} %get-tuple-element.10.slot_of, s32[16]{0:T(128)S(1)} %fusion.1.places, f32[16]{0:T(128)S(1)} %compare_convert_fusion.live_place, bf16[192,64,128]{2,1,0:T(8,128)(2,1)S(1)} %copy-done, ...), custom_call_target="tpu_custom_call" | custom-call | flops 4000000000 | bytes 8000000 | tf_op jit(solution)/shard_map/pallas_call | solution.py:532
  81.0 0.6 slice.3
  81.6 0.9 %copy.14 = f32[24,64,128]{2,1,0:T(8,128)} copy(f32[24,64,128]{2,1,0:T(8,128)S(1)} %get-tuple-element.17) | data formatting | bytes 1572864
  82.5 1.0 %copy.15 = f32[1,1,16,128,128]{4,3,2,1,0:T(8,128)} copy(f32[1,1,16,128,128]{4,3,2,1,0:T(8,128)S(1)} %bitcast.13) | data formatting | bytes 2097152
  (21 shorter events, 0.3 us)
Async XLA Ops:
  5.7 1.9 %copy-start = (bf16[192,64,128]{2,1,0:T(8,128)(2,1)S(1)}, bf16[192,64,128]{2,1,0:T(8,128)(2,1)}, u32[]{:S(2)}) copy-start(bf16[192,64,128]{2,1,0:T(8,128)(2,1)} %fields.1) | copy-start | bytes 9437188
  7.6 1.2 %copy-start.1 = (f32[1,1,16,128,128]{4,3,2,1,0:T(8,128)S(1)}, f32[1,1,16,128,128]{4,3,2,1,0:T(8,128)}, u32[]{:S(2)}) copy-start(f32[1,1,16,128,128]{4,3,2,1,0:T(8,128)} %param.11) | copy-start | bytes 3145732

commit v2 on v1

--- a/solution.py
+++ b/solution.py
@@ -96,6 +96,9 @@
 LANES = 128
 SUB = 8
 TOP = 32760.0
+RUNS = 4
+SECOND_ROW = 2
+FIRST_ROW = 4
 MESH = pl.DeviceIdType.MESH
 NT = (((1,), (1,)), ((), ()))
 
@@ -112,14 +115,15 @@
 
 def step_kernel(
     groups, owners,
-    slot_of, places, live_place,
-    fields, tcol, msg0, targets, mats,
+    first_ids, second_ids, count, labels, fields_in, mats_in,
     logits_out, grad_out, mats_out,
+    slot_of, places, fields, mats, mats_new,
     first_vec, first_t, served_vec, second_vec, mats_mid, total,
     msg1, got1, msg2, got2, term_a, term_b, send_a, send_b, got_a, got_b, err_col, acc,
-    sem_v, sem_m1, sem_m2, sem_a, sem_b,
+    sem_f, sem_m, sem_v, sem_m1, sem_m2, sem_a, sem_b,
 ):
     samples, per_block, feature = fields.shape
+    shift = per_block.bit_length() - 1
     slots = mats.shape[0]
     cap = slots // groups
     chunk = samples // owners
@@ -132,6 +136,17 @@
     inv_root = 1.0 / math.sqrt(feature)
     extra = 2 * LANES - samples
 
+    run = samples // RUNS
+
+    def load_fields(r):
+        part = pl.ds(r * run, run)
+        return pltpu.make_async_copy(fields_in.at[part], fields.at[part], sem_f.at[r])
+
+    for r in range(RUNS):
+        load_fields(r).start()
+    load_mats = pltpu.make_async_copy(mats_in, mats, sem_m.at[0])
+    load_mats.start()
+
     barrier = pltpu.get_barrier_semaphore()
 
     def greet(d, _):
@@ -143,39 +158,79 @@
 
     lax.fori_loop(1, devices, greet, 0)
 
-    def gather(lo, out):
+    def gather(spots):
         wide = SUB * per_block
-        rows = slots * SUB
-        lanes = lax.broadcasted_iota(jnp.int32, (rows, wide), 1)
-        pick = jnp.where(lanes == tcol[lo : lo + rows, :], 1.0, 0.0).astype(jnp.bfloat16)
-
-        def part(i, _):
-            halves = []
-            for h in range(2):
-                block = fields[pl.ds(i * 16 + h * SUB, SUB)].reshape(wide, feature)
-                halves.append(dot32(pick, block).reshape(slots, SUB, feature))
-            out[:, pl.ds(pl.multiple_of(i * 16, 16), 16), :] = jnp.concatenate(halves, axis=1).astype(jnp.bfloat16)
-            return 0
-
-        lax.fori_loop(0, samples // 16, part, 0)
-
-    def vec_copy(j):
+        lanes = lax.broadcasted_iota(jnp.int32, (SUB, wide), 1)
+        lanes = lanes - lax.broadcasted_iota(jnp.int32, (SUB, wide), 0) * per_block
+        pick = jnp.concatenate([jnp.where(lanes == f, 1.0, 0.0) for f in spots], axis=0).astype(jnp.bfloat16)
+
+        def rows(out, start, size):
+            def part(i, _):
+                at = pl.multiple_of(start + i * 16, 16)
+                halves = []
+                for h in range(2):
+                    block = fields[pl.ds(at + h * SUB, SUB)].reshape(wide, feature)
+                    halves.append(dot32(pick, block).reshape(slots, SUB, feature))
+                out[:, pl.ds(at, 16), :] = jnp.concatenate(halves, axis=1).astype(jnp.bfloat16)
+                return 0
+
+            lax.fori_loop(0, size // 16, part, 0)
+
+        return rows
+
+    def vec_copy(j, r):
         to = lax.rem(g + j, groups)
+        part = pl.ds(r * run, run)
         return pltpu.make_async_remote_copy(
-            src_ref=served_vec.at[pl.ds(to * cap, cap)],
-            dst_ref=second_vec.at[pl.ds(g * cap, cap)],
-            send_sem=sem_v.at[0, j],
-            recv_sem=sem_v.at[1, j],
+            src_ref=served_vec.at[pl.ds(to * cap, cap), part],
+            dst_ref=second_vec.at[pl.ds(g * cap, cap), part],
+            send_sem=sem_v.at[0, j, r],
+            recv_sem=sem_v.at[1, j, r],
             device_id=(to, o),
             device_id_type=MESH,
         )
 
-    gather(slots * SUB, served_vec)
-    pl.semaphore_wait(barrier, devices - 1)
-    for j in range(1, groups):
-        vec_copy(j).start()
+    served = []
+    for q in range(groups):
+        found, seen = [jnp.int32(0)] * cap, jnp.int32(0)
+        for s in range(slots):
+            field = second_ids[q, 0, s]
+            hit = (field >> shift) == g
+            found = [
+                jnp.where(jnp.logical_and(hit, seen == c), field & (per_block - 1), f) for c, f in enumerate(found)
+            ]
+            seen = seen + hit.astype(jnp.int32)
+        served += found
+    gather_served = gather(served)
+    for r in range(RUNS):
+        load_fields(r).wait()
+        gather_served(served_vec, r * run, run)
+        if r == 0:
+            pl.semaphore_wait(barrier, devices - 1)
+        for j in range(1, groups):
+            vec_copy(j, r).start()
     second_vec[pl.ds(g * cap, cap)] = served_vec[pl.ds(g * cap, cap)]
-    gather(0, first_vec)
+
+    owner_of = [jnp.int32(0)] * slots
+    seen = [jnp.int32(0)] * groups
+    for s in range(slots):
+        block = second_ids[g, 0, s] >> shift
+        place = jnp.int32(0)
+        for q in range(groups):
+            hit = block == q
+            place = jnp.where(hit, q * cap + seen[q], place)
+            seen[q] = seen[q] + hit.astype(jnp.int32)
+        places[s] = place
+        owner_of = [jnp.where(place == p, s, t) for p, t in enumerate(owner_of)]
+    for p in range(slots):
+        slot_of[p] = owner_of[p]
+    first_at = [first_ids[0, 0, t] - g * per_block for t in owner_of]
+    second_at = [second_ids[g, 0, t] & (per_block - 1) for t in owner_of]
+
+    def live_of(p):
+        return jnp.where(slot_of[p] < count[0, 0], 1.0, 0.0)
+
+    gather(first_at)(first_vec, 0, samples)
 
     def turn(p, _):
         v = first_vec[p].astype(jnp.float32)
@@ -196,12 +251,14 @@
         for c in range(cap):
             p = q * cap + c
             mixed, _, _ = mix(p, mats[slot_of[p]])
-            sums = sums + (mixed * second_vec[p].astype(jnp.float32)) * live_place[p]
+            sums = sums + (mixed * second_vec[p].astype(jnp.float32)) * live_of(p)
         total[...] = sums
 
+    load_mats.wait()
     first_pass(g)
     for j in range(1, groups):
-        vec_copy(j).wait_recv()
+        for r in range(RUNS):
+            vec_copy(j, r).wait_recv()
         first_pass(lax.rem(g + groups - j, groups))
 
     def partial_rows():
@@ -213,9 +270,24 @@
         ]
 
     row_id = lax.broadcasted_iota(jnp.int32, (SUB, LANES), 0)
+    lane_id = lax.broadcasted_iota(jnp.int32, (SUB, LANES), 1)
+    segment = cap * SUB
+    span = LANES // segment
+
+    def spot_row(ids, q):
+        spots = jnp.zeros((SUB, LANES), jnp.int32)
+        for c in range(cap):
+            spots = jnp.where((lane_id % segment) // SUB == c, ids[q * cap + c], spots)
+        spots = spots + (lane_id % SUB) * per_block
+        return jnp.where(lane_id // segment == lax.rem(o, span), spots, 0).astype(jnp.float32)
+
+    tables = jnp.zeros((SUB, LANES), jnp.float32)
+    for q in range(groups):
+        tables = jnp.where(row_id == FIRST_ROW + q, spot_row(first_at, q), tables)
     r0, r1 = partial_rows()
+    tables = jnp.where(row_id == 0, r0, jnp.where(row_id == 1, r1, tables))
     for q in range(groups):
-        msg1[q] = jnp.where(row_id == 0, r0, jnp.where(row_id == 1, r1, msg0[q]))
+        msg1[q] = jnp.where(row_id == SECOND_ROW, spot_row(second_at, q), tables)
 
     def tile_copy(src, dst, sems, d, pick_own):
         peer = lax.rem(me + d, devices)
@@ -254,13 +326,22 @@
 
         lax.fori_loop(1, devices, one, 0)
 
+    wanted = labels[...].astype(jnp.float32)
+    targets = jnp.concatenate(
+        [
+            wanted[:, 0:LANES],
+            jnp.concatenate([wanted[:, LANES:samples], jnp.zeros((1, extra), jnp.float32)], axis=1),
+        ],
+        axis=0,
+    )
+
     def errors_of(got, at):
         sums = got[0]
         for d in range(1, devices):
             sums = sums + got[d]
         sums = sums[at : at + 2] * (1.0 / feature)
         logits = logit_scale * sums
-        return logits, jax.nn.sigmoid(logits) - targets[0:2]
+        return logits, jax.nn.sigmoid(logits) - targets
 
     def error_row(err):
         return jnp.concatenate([err[0:1], err[1:2, 0 : samples - LANES]], axis=1)
@@ -284,7 +365,7 @@
         sums = total[...]
         for c in range(cap):
             p = q * cap + c
-            live = live_place[p]
+            live = live_of(p)
             mid = mats[slot_of[p]] - (rate * live) * gradient(p, erow)
             mats_mid[p] = mid
             mixed, high, low = mix(p, mid)
@@ -345,24 +426,26 @@
     got_b[g, o] = send_b[g, o]
     send_units(0)
 
-    def middle(j, _):
+    def later(j, _):
         second_pass(j)
-        send_units(j)
-        unit_b(j, 0).start()
-        return 0
-
-    lax.fori_loop(1, groups - 1, middle, 0)
-    second_pass(groups - 1)
+        return 0
+
+    lax.fori_loop(1, groups, later, 0)
     r0, r1 = partial_rows()
     for w in range(owners):
         msg2[w] = jnp.where(row_id == groups, r0, jnp.where(row_id == groups + 1, r1, msg2[w]))
     send_tiles(msg2, got2, sem_m2, True)
-    send_units(groups - 1)
-    unit_b(groups - 1, 0).start()
+
+    def send_later(j, _):
+        unit_b(j, 0).start()
+        send_units(j)
+        return 0
+
+    lax.fori_loop(1, groups, send_later, 0)
     got2[me] = msg2[o]
     wait_tiles(msg2, got2, sem_m2)
     logits, err = errors_of(got2, groups)
-    logits_out[...] = jnp.concatenate([logits, jnp.zeros((SUB - 2, LANES), jnp.float32)], axis=0)
+    logits_out[...] = error_row(logits)
     erow = error_row(err)
     eye = lax.broadcasted_iota(jnp.int32, (LANES, LANES), 0) == lax.broadcasted_iota(jnp.int32, (LANES, LANES), 1)
     for half in range(2):
@@ -371,10 +454,12 @@
 
     def last_update(s, _):
         p = places[s]
-        mats_out[s] = mats_mid[p] - (rate * live_place[p]) * gradient(p, erow)
+        mats_new[s] = mats_mid[p] - (rate * live_of(p)) * gradient(p, erow)
         return 0
 
     lax.fori_loop(0, slots, last_update, 0)
+    store_mats = pltpu.make_async_copy(mats_new, mats_out, sem_m.at[0])
+    store_mats.start()
 
     col = err_col[pl.ds(pl.multiple_of(o * chunk, SUB), chunk), :]
     parts = chunk // SUB
@@ -389,79 +474,64 @@
             out.append((w >> 16).astype(jnp.float32) * factor)
         return out
 
-    def place_terms(terms, spots, fresh=False):
+    def pick_of(spots):
         spots = (spots + 0.5).astype(jnp.int32)
         pick = jnp.where(field_rows == spots, 1.0, 0.0).astype(jnp.bfloat16)
+        return [pick, pick]
+
+    def rows_of(terms):
         x = jnp.concatenate(
             [jnp.concatenate([t[i * SUB : (i + 1) * SUB] for t in terms], axis=0) for i in range(parts)], axis=1
         )
-        high, low = two_parts(x)
-        out = dot32(jnp.concatenate([pick, pick], axis=1), jnp.concatenate([high, low], axis=0))
-        acc[...] = out if fresh else acc[...] + out
-
-    span = LANES // (cap * SUB)
+        return list(two_parts(x))
+
+    def wait_a(q, w):
+        pltpu.make_async_remote_copy(
+            src_ref=send_a.at[q, w], dst_ref=got_a.at[w, q], send_sem=sem_a.at[0, q, w],
+            recv_sem=sem_a.at[1, q, w], device_id=(g, w), device_id_type=MESH,
+        ).wait_recv()
+
+    def wait_b(q, w):
+        pltpu.make_async_remote_copy(
+            src_ref=send_b.at[q, w], dst_ref=got_b.at[q, w], send_sem=sem_b.at[0, q, w],
+            recv_sem=sem_b.at[1, q, w], device_id=(q, w), device_id_type=MESH,
+        ).wait_recv()
 
     acc[...] = jnp.zeros_like(acc)
 
-    def arrive_b(j, k):
-        @pl.when(j + k > 0)
-        def _():
-            q, w = lax.rem(g + groups - j, groups), lax.rem(o + owners - k, owners)
-            pltpu.make_async_remote_copy(
-                src_ref=send_b.at[q, w], dst_ref=got_b.at[q, w], send_sem=sem_b.at[0, q, w],
-                recv_sem=sem_b.at[1, q, w], device_id=(q, w), device_id_type=MESH,
-            ).wait_recv()
-
-    def from_seconds(j, _):
-        q = lax.rem(g + groups - j, groups)
-
-        def one(k, _):
-            arrive_b(j, k)
-            return 0
-
-        lax.fori_loop(0, owners, one, 0)
-
-        def half(h, _):
-            terms, spots = [], 0.0
-            for i in range(span):
-                w = h * span + i
-                src = q * owners + w
-                scale = got2[src, pl.ds(g, 1), :]
-                terms += decode(lambda k: got_b[q, w, pl.ds(k * chunk, chunk), :], scale)
-                spots = spots + got1[src][3:4]
-            place_terms(terms, spots)
-            return 0
-
-        lax.fori_loop(0, owners // span, half, 0)
-        return 0
-
-    lax.fori_loop(0, groups, from_seconds, 0)
-
-    def from_firsts(k, _):
-        w = lax.rem(o + owners - k, owners)
-        src = g * owners + w
-
-        @pl.when(k > 0)
-        def _():
-            for q in range(groups):
-                pltpu.make_async_remote_copy(
-                    src_ref=send_a.at[q, w], dst_ref=got_a.at[w, q], send_sem=sem_a.at[0, q, w],
-                    recv_sem=sem_a.at[1, q, w], device_id=(g, w), device_id_type=MESH,
-                ).wait_recv()
-
-        terms = []
-        for q in range(groups):
-            scale = got2[src][q : q + 1]
-            terms += decode(lambda m: got_a[w, q, pl.ds(m * chunk, chunk), :], scale)
-        place_terms(terms, got1[src][2:3])
-        return 0
-
-    lax.fori_loop(0, owners, from_firsts, 0)
+    def arrivals(n, _):
+        j, h = n // (owners // span), n % (owners // span)
+        qa, qb = lax.rem(g + j, groups), lax.rem(g + groups - j, groups)
+        terms_a, terms_b, spots_a, spots_b = [], [], 0.0, 0.0
+        for i in range(span):
+            k = h * span + lax.rem(o + span - i, span)
+            w = lax.rem(o + owners - k, owners)
+
+            @pl.when(k > 0)
+            def _():
+                wait_a(qa, w)
+
+            @pl.when(j + k > 0)
+            def _():
+                wait_b(qb, w)
+
+            scale = got2[g * owners + w, pl.ds(qa, 1), :]
+            terms_a += decode(lambda m: got_a[w, qa, pl.ds(m * chunk, chunk), :], scale)
+            spots_a = spots_a + got1[g * owners + w, pl.ds(FIRST_ROW + qa, 1), :]
+            scale = got2[qb * owners + w, pl.ds(g, 1), :]
+            terms_b += decode(lambda m: got_b[qb, w, pl.ds(m * chunk, chunk), :], scale)
+            spots_b = spots_b + got1[qb * owners + w][SECOND_ROW : SECOND_ROW + 1]
+        pick = jnp.concatenate(pick_of(spots_a) + pick_of(spots_b), axis=1)
+        acc[...] += dot32(pick, jnp.concatenate(rows_of(terms_a) + rows_of(terms_b), axis=0))
+        return 0
+
+    lax.fori_loop(0, groups * (owners // span), arrivals, 0)
     for i in range(parts):
         grad_out[i * SUB : (i + 1) * SUB] = acc[:, i * feature : (i + 1) * feature].reshape(SUB, per_block, feature)
 
     for j in range(1, groups):
-        vec_copy(j).wait_send()
+        for r in range(RUNS):
+            vec_copy(j, r).wait_send()
 
     def drain_tiles(d, _):
         tile_copy(msg1, got1, sem_m1, d, False).wait_send()
@@ -485,60 +555,37 @@
         return 0
 
     lax.fori_loop(0, groups, drain_units, 0)
+    store_mats.wait()
 
 
 def on_device_kernel(fields, labels, pair_first, pair_second, pair_count, pair_mats):
     groups = lax.axis_size("grp")
     owners = lax.axis_size("own")
-    g, o = lax.axis_index("grp"), lax.axis_index("own")
     samples, per_block, feature = fields.shape
     slots = pair_first.shape[2]
     cap = slots // groups
     chunk = samples // owners
     devices = groups * owners
-    table = pair_second[:, 0, :]
-    block_ids = table // per_block
-    offsets = table % per_block
-    same = block_ids[:, :, None] == block_ids[:, None, :]
-    slot_iota = jnp.arange(slots, dtype=jnp.int32)
-    before = slot_iota[None, :] < slot_iota[:, None]
-    ranks = jnp.sum((same & before[None]).astype(jnp.int32), axis=2)
-    places_all = block_ids * cap + ranks
-    match = places_all[:, :, None] == slot_iota[None, None, :]
-    off_place = jnp.sum(jnp.where(match, offsets[:, :, None], 0), axis=1)
-    served = lax.dynamic_slice_in_dim(off_place, g * cap, cap, axis=1).reshape(-1)
-    places = lax.dynamic_index_in_dim(places_all, g, 0, keepdims=False)
-    mine = places[:, None] == slot_iota[None, :]
-    slot_of = jnp.sum(jnp.where(mine, slot_iota[:, None], 0), axis=0)
-    first_local = pair_first[0, 0] - g * per_block
-    first_place = jnp.sum(jnp.where(mine, first_local[:, None], 0), axis=0)
-    second_place = lax.dynamic_index_in_dim(off_place, g, 0, keepdims=False)
-    live_place = (slot_of < pair_count[0, 0]).astype(jnp.float32)
-    lift = jnp.arange(SUB, dtype=jnp.int32) * per_block
-    spots = lambda idx: (idx[:, None] + lift[None, :]).reshape(-1)
-    tcol = spots(jnp.concatenate([first_place, served]))[:, None]
-    span = LANES // (cap * SUB)
-    segments = jnp.tile(spots(second_place).reshape(groups, cap * SUB), (1, span))
-    lane_seg = jnp.arange(LANES, dtype=jnp.int32) // (cap * SUB)
-    segments = jnp.where(lane_seg[None, :] == o % span, segments, 0)
-    firsts = jnp.broadcast_to(spots(first_place)[None], (groups, LANES))
-    zero = jnp.zeros((groups, 2, LANES), jnp.int32)
-    msg0 = jnp.concatenate([zero, firsts[:, None], segments[:, None], zero, zero], axis=1).astype(jnp.float32)
-    targets = jnp.pad(labels.astype(jnp.float32), (0, SUB * LANES - samples)).reshape(SUB, LANES)
     smem = pl.BlockSpec(memory_space=pltpu.SMEM)
     vmem = pl.BlockSpec(memory_space=pltpu.VMEM)
+    hbm = pl.BlockSpec(memory_space=pl.ANY)
     rows = cap // 2 * chunk
     f32, bf16, i32 = jnp.float32, jnp.bfloat16, jnp.int32
     logits, grad, new_mats = pl.pallas_call(
         functools.partial(step_kernel, groups, owners),
         out_shape=(
-            jax.ShapeDtypeStruct((SUB, LANES), f32),
+            jax.ShapeDtypeStruct((1, samples), f32),
             jax.ShapeDtypeStruct((chunk, per_block, feature), f32),
             jax.ShapeDtypeStruct((slots, feature, feature), f32),
         ),
-        in_specs=[smem] * 3 + [vmem] * 5,
-        out_specs=(vmem,) * 3,
+        in_specs=[smem] * 3 + [vmem] + [hbm] * 2,
+        out_specs=(vmem, vmem, hbm),
         scratch_shapes=[
+            pltpu.SMEM((slots,), i32),
+            pltpu.SMEM((slots,), i32),
+            pltpu.VMEM(fields.shape, bf16),
+            pltpu.VMEM((slots, feature, feature), f32),
+            pltpu.VMEM((slots, feature, feature), f32),
             pltpu.VMEM((slots, samples, feature), bf16),
             pltpu.VMEM((slots, feature, 2 * LANES), bf16),
             pltpu.VMEM((slots, samples, feature), bf16),
@@ -557,18 +604,20 @@
             pltpu.VMEM((groups, owners, rows, feature), i32),
             pltpu.VMEM((2 * LANES, LANES), f32),
             pltpu.VMEM((SUB * per_block, chunk // SUB * feature), f32),
-            pltpu.SemaphoreType.DMA((2, groups)),
+            pltpu.SemaphoreType.DMA((RUNS,)),
+            pltpu.SemaphoreType.DMA((1,)),
+            pltpu.SemaphoreType.DMA((2, groups, RUNS)),
             pltpu.SemaphoreType.DMA((2, devices)),
             pltpu.SemaphoreType.DMA((2, devices)),
             pltpu.SemaphoreType.DMA((2, groups, owners)),
             pltpu.SemaphoreType.DMA((2, groups, owners)),
         ],
         compiler_params=pltpu.CompilerParams(
-            collective_id=0, has_side_effects=True, vmem_limit_bytes=40 * 1024 * 1024
+            collective_id=0, has_side_effects=True, vmem_limit_bytes=56 * 1024 * 1024
         ),
         cost_estimate=pl.CostEstimate(flops=4 * 10**9, bytes_accessed=8 * 10**6, transcendentals=400),
-    )(slot_of, places, live_place, fields, tcol, msg0, targets, pair_mats[0, 0])
-    return (logits.reshape(-1)[:samples], grad, new_mats[None, None])
+    )(pair_first, pair_second, pair_count, labels.reshape(1, samples), fields, pair_mats[0, 0])
+    return (logits.reshape(samples), grad, new_mats[None, None])
 
 
 def fits(groups, owners, fields, pair_first):
@@ -582,9 +631,10 @@
         and cap % 2 == 0
         and LANES < samples <= 2 * LANES
         and samples % (SUB * owners) == 0
-        and samples % 16 == 0
+        and samples % (16 * RUNS) == 0
+        and fields.shape[1] & (fields.shape[1] - 1) == 0
         and owners % (LANES // (cap * SUB)) == 0
-        and groups + 2 <= SUB
+        and FIRST_ROW + groups <= SUB
     )
 
 

time: 83.7 us -> 74.2 us (0.89)
  Pallas kernels: 72.2 us -> 67.1 us
  other arithmetic: 3.47 us -> 0 us
    pallas_call x1, Pallas kernels: 72.2 us -> 67.1 us  [on_device_kernel(): pl.pallas_call(functools.partial(step_kernel, groups, owners), out_shape=...]
    select_n x3 -> x0, other arithmetic: 1.4 us -> none  [the longest x1 0.7 us: on_device_kernel(): block_ids = table // per_block]
    unnamed x6 -> x3, local copies, waits for them, and re-layouts: 4.96 us -> 5.62 us
where the time goes in v2:
time: 74.2 us; the launch traced here: 74 us
  Pallas kernels  67.1 us (90%)
  local copies, waits for them, and re-layouts  5.62 us (8%)
  between operations  1.29 us (2%)
    pallas_call x1, Pallas kernels, on_device_kernel(): pl.pallas_call(functools.partial(step_kernel, groups, owners), out_shape=...  67.1 us
    unnamed x3, local copies, waits for them, and re-layouts  5.62 us

profile of v2, /device:TPU:0, one launch (start us, length us, event | category | flops | bytes accessed | tf_op | source)
XLA Modules:
  0.0 74.0 jit_solution(18291035443410129657)
XLA Ops:
  1.3 67.1 %shard_map.85 = (f32[1,192]{1,0:T(1,128)}, f32[24,64,128]{2,1,0:T(8,128)}, f32[16,128,128]{2,1,0:T(8,128)}) custom-call(s32[1,1,16]{2,1,0:T(1,128)} %first_ids.1, s32[4,1,16]{2,1,0:T(1,128)} %second_ids.1, s32[1,1]{1,0:T(1,128)S(6)} %copy.12.count, s32[1,192]{1,0:T(1,128)} %bitcast.7, bf16[192,64,128]{2,1,0:T(8,128)(2,1)} %fields_in.1, f32[16,128,128]{2,1,0:T(8,128)} %bitcast.6), custom_call_target="tpu_custom_call" | custom-call | flops 4000000000 | bytes 8000000 | tf_op jit(solution)/shard_map/pallas_call | solution.py:574
  68.4 1.2 %copy.13 = f32[192]{0:T(256)} copy(f32[192]{0:T(256)} %bitcast.5) | data formatting | bytes 1536
  69.6 2.1 %copy.14 = f32[24,64,128]{2,1,0:T(8,128)} copy(f32[24,64,128]{2,1,0:T(8,128)} %get-tuple-element.13) | data formatting | bytes 1572864
  71.7 2.3 %copy.15 = f32[1,1,16,128,128]{4,3,2,1,0:T(8,128)} copy(f32[1,1,16,128,128]{4,3,2,1,0:T(8,128)} %bitcast.4) | data formatting | bytes 2097152

commit v3 on v2

--- a/solution.py
+++ b/solution.py
@@ -117,7 +117,7 @@
     groups, owners,
     first_ids, second_ids, count, labels, fields_in, mats_in,
     logits_out, grad_out, mats_out,
-    slot_of, places, fields, mats, mats_new,
+    slot_of, places, fields, mats,
     first_vec, first_t, served_vec, second_vec, mats_mid, total,
     msg1, got1, msg2, got2, term_a, term_b, send_a, send_b, got_a, got_b, err_col, acc,
     sem_f, sem_m, sem_v, sem_m1, sem_m2, sem_a, sem_b,
@@ -398,27 +398,33 @@
 
         lax.fori_loop(0, owners, code, 0)
 
+    def partner(k):
+        w, bit = o, 1
+        while bit < owners:
+            w = w + ((k // bit) % 2) * (bit - 2 * bit * ((w // bit) % 2))
+            bit *= 2
+        return w
+
+    order = [k for pair in zip(range(owners // 2, owners), [*range(1, owners // 2), 0]) for k in pair if k]
+
     def unit_a(j, k):
-        q, w = lax.rem(g + j, groups), lax.rem(o + k, owners)
+        q, w = lax.rem(g + j, groups), partner(k)
         return pltpu.make_async_remote_copy(
             src_ref=send_a.at[q, w], dst_ref=got_a.at[o, q], send_sem=sem_a.at[0, q, w],
             recv_sem=sem_a.at[1, q, o], device_id=(g, w), device_id_type=MESH,
         )
 
     def unit_b(j, k):
-        q, w = lax.rem(g + j, groups), lax.rem(o + k, owners)
+        q, w = lax.rem(g + j, groups), partner(k)
         return pltpu.make_async_remote_copy(
             src_ref=send_b.at[q, w], dst_ref=got_b.at[g, o], send_sem=sem_b.at[0, q, w],
             recv_sem=sem_b.at[1, g, o], device_id=(q, w), device_id_type=MESH,
         )
 
     def send_units(j):
-        def one(k, _):
+        for k in order:
             unit_a(j, k).start()
             unit_b(j, k).start()
-            return 0
-
-        lax.fori_loop(1, owners, one, 0)
         q = lax.rem(g + j, groups)
         got_a[o, q] = send_a[q, o]
 
@@ -454,12 +460,10 @@
 
     def last_update(s, _):
         p = places[s]
-        mats_new[s] = mats_mid[p] - (rate * live_of(p)) * gradient(p, erow)
+        mats_out[s] = mats_mid[p] - (rate * live_of(p)) * gradient(p, erow)
         return 0
 
     lax.fori_loop(0, slots, last_update, 0)
-    store_mats = pltpu.make_async_copy(mats_new, mats_out, sem_m.at[0])
-    store_mats.start()
 
     col = err_col[pl.ds(pl.multiple_of(o * chunk, SUB), chunk), :]
     parts = chunk // SUB
@@ -504,8 +508,8 @@
         qa, qb = lax.rem(g + j, groups), lax.rem(g + groups - j, groups)
         terms_a, terms_b, spots_a, spots_b = [], [], 0.0, 0.0
         for i in range(span):
-            k = h * span + lax.rem(o + span - i, span)
-            w = lax.rem(o + owners - k, owners)
+            k = h * span + partner(i) % span
+            w = partner(k)
 
             @pl.when(k > 0)
             def _():
@@ -555,7 +559,6 @@
         return 0
 
     lax.fori_loop(0, groups, drain_units, 0)
-    store_mats.wait()
 
 
 def on_device_kernel(fields, labels, pair_first, pair_second, pair_count, pair_mats):
@@ -568,7 +571,7 @@
     devices = groups * owners
     smem = pl.BlockSpec(memory_space=pltpu.SMEM)
     vmem = pl.BlockSpec(memory_space=pltpu.VMEM)
-    hbm = pl.BlockSpec(memory_space=pl.ANY)
+    hbm = pl.BlockSpec(memory_space=pltpu.HBM)
     rows = cap // 2 * chunk
     f32, bf16, i32 = jnp.float32, jnp.bfloat16, jnp.int32
     logits, grad, new_mats = pl.pallas_call(
@@ -579,12 +582,11 @@
             jax.ShapeDtypeStruct((slots, feature, feature), f32),
         ),
         in_specs=[smem] * 3 + [vmem] + [hbm] * 2,
-        out_specs=(vmem, vmem, hbm),
+        out_specs=(vmem,) * 3,
         scratch_shapes=[
             pltpu.SMEM((slots,), i32),
             pltpu.SMEM((slots,), i32),
             pltpu.VMEM(fields.shape, bf16),
-            pltpu.VMEM((slots, feature, feature), f32),
             pltpu.VMEM((slots, feature, feature), f32),
             pltpu.VMEM((slots, samples, feature), bf16),
             pltpu.VMEM((slots, feature, 2 * LANES), bf16),
@@ -613,7 +615,7 @@
             pltpu.SemaphoreType.DMA((2, groups, owners)),
         ],
         compiler_params=pltpu.CompilerParams(
-            collective_id=0, has_side_effects=True, vmem_limit_bytes=56 * 1024 * 1024
+            collective_id=0, has_side_effects=True, vmem_limit_bytes=52 * 1024 * 1024
         ),
         cost_estimate=pl.CostEstimate(flops=4 * 10**9, bytes_accessed=8 * 10**6, transcendentals=400),
     )(pair_first, pair_second, pair_count, labels.reshape(1, samples), fields, pair_mats[0, 0])
@@ -633,6 +635,7 @@
         and samples % (SUB * owners) == 0
         and samples % (16 * RUNS) == 0
         and fields.shape[1] & (fields.shape[1] - 1) == 0
+        and owners & (owners - 1) == 0
         and owners % (LANES // (cap * SUB)) == 0
         and FIRST_ROW + groups <= SUB
     )

time: 74.2 us -> 73.2 us (0.987)
  local copies, waits for them, and re-layouts: 5.62 us -> 4.42 us
    unnamed x3 -> x9, local copies, waits for them, and re-layouts: 5.62 us -> 4.42 us
where the time goes in v3:
time: 73.2 us; the launch traced here: 73 us
  Pallas kernels  67.3 us (92%)
  local copies, waits for them, and re-layouts  4.42 us (6%)
  between operations  1.3 us (2%)
    pallas_call x1, Pallas kernels, on_device_kernel(): pl.pallas_call(functools.partial(step_kernel, groups, owners), out_shape=...  67.3 us
    unnamed x9, local copies, waits for them, and re-layouts  4.42 us

profile of v3, /device:TPU:0, one launch (start us, length us, event | category | flops | bytes accessed | tf_op | source)
XLA Modules:
  0.0 73.0 jit_solution(16693647814895551255)
XLA Ops:
  1.3 0.0 copy-start
  1.3 0.7 copy-done
  2.0 0.0 copy-start.1
  2.0 0.7 copy-done.1
  2.6 0.0 copy-start.2
  2.6 0.7 copy-done.2
  3.3 67.3 %shard_map.85 = (f32[1,192]{1,0:T(1,128)S(1)}, f32[24,64,128]{2,1,0:T(8,128)S(1)}, f32[16,128,128]{2,1,0:T(8,128)S(1)}) custom-call(s32[1,1,16]{2,1,0:T(1,128)S(1)} %copy-done.2, s32[4,1,16]{2,1,0:T(1,128)S(1)} %copy-done, s32[1,1]{1,0:T(1,128)S(6)} %copy.12.count, s32[1,192]{1,0:T(1,128)S(1)} %bitcast.6, bf16[192,64,128]{2,1,0:T(8,128)(2,1)} %fields_in.1, ...), custom_call_target="tpu_custom_call" | custom-call | flops 4000000000 | bytes 8000000 | tf_op jit(solution)/shard_map/pallas_call | solution.py:577
  70.6 0.6 copy.13
  71.1 0.9 %copy.14 = f32[24,64,128]{2,1,0:T(8,128)} copy(f32[24,64,128]{2,1,0:T(8,128)S(1)} %get-tuple-element.13) | data formatting | bytes 1572864
  72.0 1.0 %copy.15 = f32[1,1,16,128,128]{4,3,2,1,0:T(8,128)} copy(f32[1,1,16,128,128]{4,3,2,1,0:T(8,128)S(1)} %bitcast.4) | data formatting | bytes 2097152
Async XLA Ops:
  1.3 0.7 copy-start
  2.0 0.7 copy-start.1
  2.6 0.7 copy-start.2

commit v4 on v3

--- a/solution.py
+++ b/solution.py
@@ -97,6 +97,7 @@
 SUB = 8
 TOP = 32760.0
 RUNS = 4
+EARLY = 2
 SECOND_ROW = 2
 FIRST_ROW = 4
 MESH = pl.DeviceIdType.MESH
@@ -115,7 +116,7 @@
 
 def step_kernel(
     groups, owners,
-    first_ids, second_ids, count, labels, fields_in, mats_in,
+    small, small_vec, fields_in, mats_in,
     logits_out, grad_out, mats_out,
     slot_of, places, fields, mats,
     first_vec, first_t, served_vec, second_vec, mats_mid, total,
@@ -123,6 +124,9 @@
     sem_f, sem_m, sem_v, sem_m1, sem_m2, sem_a, sem_b,
 ):
     samples, per_block, feature = fields.shape
+    first_base = 2 * LANES
+    second_base = first_base + mats.shape[0]
+    count_at = second_base + groups * mats.shape[0]
     shift = per_block.bit_length() - 1
     slots = mats.shape[0]
     cap = slots // groups
@@ -194,7 +198,7 @@
     for q in range(groups):
         found, seen = [jnp.int32(0)] * cap, jnp.int32(0)
         for s in range(slots):
-            field = second_ids[q, 0, s]
+            field = small[0, second_base + q * slots + s]
             hit = (field >> shift) == g
             found = [
                 jnp.where(jnp.logical_and(hit, seen == c), field & (per_block - 1), f) for c, f in enumerate(found)
@@ -214,7 +218,7 @@
     owner_of = [jnp.int32(0)] * slots
     seen = [jnp.int32(0)] * groups
     for s in range(slots):
-        block = second_ids[g, 0, s] >> shift
+        block = small[0, second_base + g * slots + s] >> shift
         place = jnp.int32(0)
         for q in range(groups):
             hit = block == q
@@ -224,11 +228,11 @@
         owner_of = [jnp.where(place == p, s, t) for p, t in enumerate(owner_of)]
     for p in range(slots):
         slot_of[p] = owner_of[p]
-    first_at = [first_ids[0, 0, t] - g * per_block for t in owner_of]
-    second_at = [second_ids[g, 0, t] & (per_block - 1) for t in owner_of]
+    first_at = [small[0, first_base + t] - g * per_block for t in owner_of]
+    second_at = [small[0, second_base + g * slots + t] & (per_block - 1) for t in owner_of]
 
     def live_of(p):
-        return jnp.where(slot_of[p] < count[0, 0], 1.0, 0.0)
+        return jnp.where(slot_of[p] < small[0, count_at], 1.0, 0.0)
 
     gather(first_at)(first_vec, 0, samples)
 
@@ -241,17 +245,16 @@
     lax.fori_loop(0, slots, turn, 0)
     total[...] = jnp.zeros_like(total)
 
-    def mix(p, mat):
-        v1 = first_vec[p]
-        high, low = two_parts(mat)
-        return dot32(jnp.concatenate([v1, v1], axis=1), jnp.concatenate([high, low], axis=0)), high, low
-
     def first_pass(q):
+        spots = [q * cap + c for c in range(cap)]
+        split = [two_parts(mats[slot_of[p]]) for p in spots]
+        firsts = [first_vec[p] for p in spots]
+        mixed = [
+            dot32(jnp.concatenate([v, v], axis=1), jnp.concatenate(parts, axis=0)) for v, parts in zip(firsts, split)
+        ]
         sums = total[...]
-        for c in range(cap):
-            p = q * cap + c
-            mixed, _, _ = mix(p, mats[slot_of[p]])
-            sums = sums + (mixed * second_vec[p].astype(jnp.float32)) * live_of(p)
+        for m, p in zip(mixed, spots):
+            sums = sums + (m * second_vec[p].astype(jnp.float32)) * live_of(p)
         total[...] = sums
 
     load_mats.wait()
@@ -326,14 +329,7 @@
 
         lax.fori_loop(1, devices, one, 0)
 
-    wanted = labels[...].astype(jnp.float32)
-    targets = jnp.concatenate(
-        [
-            wanted[:, 0:LANES],
-            jnp.concatenate([wanted[:, LANES:samples], jnp.zeros((1, extra), jnp.float32)], axis=1),
-        ],
-        axis=0,
-    )
+    targets = jnp.concatenate([small_vec[:, 0:LANES], small_vec[:, LANES : 2 * LANES]], axis=0).astype(jnp.float32)
 
     def errors_of(got, at):
         sums = got[0]
@@ -346,11 +342,11 @@
     def error_row(err):
         return jnp.concatenate([err[0:1], err[1:2, 0 : samples - LANES]], axis=1)
 
-    def gradient(p, erow):
-        v = first_t[p][:, 0:samples].astype(jnp.float32) * erow
-        high, low = two_parts(v)
-        v2 = second_vec[p]
-        return dot32(high, v2) + dot32(low, v2)
+    def gradients(spots, erow):
+        turned = [first_t[p][:, 0:samples].astype(jnp.float32) * erow for p in spots]
+        both = [jnp.concatenate(two_parts(v), axis=0) for v in turned]
+        out = [dot32(v, second_vec[p]) for v, p in zip(both, spots)]
+        return [x[0:feature] + x[feature:] for x in out]
 
     send_tiles(msg1, got1, sem_m1, False)
     got1[me] = msg1[g]
@@ -362,25 +358,35 @@
 
     def second_pass(j):
         q = lax.rem(g + j, groups)
-        sums = total[...]
-        for c in range(cap):
-            p = q * cap + c
-            live = live_of(p)
-            mid = mats[slot_of[p]] - (rate * live) * gradient(p, erow)
-            mats_mid[p] = mid
-            mixed, high, low = mix(p, mid)
-            v2 = second_vec[p]
-            first = lax.dot_general(
-                jnp.concatenate([v2, v2], axis=1),
-                jnp.concatenate([high, low], axis=1),
+        spots = [q * cap + c for c in range(cap)]
+        lives = [live_of(p) for p in spots]
+        old = [mats[slot_of[p]] for p in spots]
+        firsts = [first_vec[p] for p in spots]
+        seconds = [second_vec[p] for p in spots]
+        moves = gradients(spots, erow)
+        mids = [m - (rate * live) * d for m, d, live in zip(old, moves, lives)]
+        split = [two_parts(m) for m in mids]
+        mixed = [
+            dot32(jnp.concatenate([v, v], axis=1), jnp.concatenate(parts, axis=0)) for v, parts in zip(firsts, split)
+        ]
+        back = [
+            lax.dot_general(
+                jnp.concatenate([v, v], axis=1),
+                jnp.concatenate(parts, axis=1),
                 NT,
                 preferred_element_type=jnp.float32,
             )
-            sums = sums + (mixed * v2.astype(jnp.float32)) * live
-            factor = live * inv_root
-            term_a[c] = first * factor
-            term_b[c] = mixed * factor
+            for v, parts in zip(seconds, split)
+        ]
+        sums = total[...]
+        for m, v, live in zip(mixed, seconds, lives):
+            sums = sums + (m * v.astype(jnp.float32)) * live
         total[...] = sums
+        for c, p in enumerate(spots):
+            factor = lives[c] * inv_root
+            mats_mid[p] = mids[c]
+            term_a[c] = back[c] * factor
+            term_b[c] = mixed[c] * factor
 
         def code(w, _):
             rows = pl.ds(pl.multiple_of(w * chunk, SUB), chunk)
@@ -434,6 +440,12 @@
 
     def later(j, _):
         second_pass(j)
+
+        @pl.when(j < EARLY)
+        def _():
+            unit_b(j, 0).start()
+            send_units(j)
+
         return 0
 
     lax.fori_loop(1, groups, later, 0)
@@ -447,7 +459,7 @@
         send_units(j)
         return 0
 
-    lax.fori_loop(1, groups, send_later, 0)
+    lax.fori_loop(EARLY, groups, send_later, 0)
     got2[me] = msg2[o]
     wait_tiles(msg2, got2, sem_m2)
     logits, err = errors_of(got2, groups)
@@ -458,12 +470,15 @@
         column = jnp.sum(jnp.where(eye, err[half : half + 1], 0.0), axis=1, keepdims=True)
         err_col[pl.ds(half * LANES, LANES), :] = jnp.broadcast_to(column, (LANES, LANES))
 
-    def last_update(s, _):
-        p = places[s]
-        mats_out[s] = mats_mid[p] - (rate * live_of(p)) * gradient(p, erow)
-        return 0
-
-    lax.fori_loop(0, slots, last_update, 0)
+    def last_update(n, _):
+        spots = [places[n * cap + c] for c in range(cap)]
+        moves = gradients(spots, erow)
+        news = [mats_mid[p] - (rate * live_of(p)) * d for p, d in zip(spots, moves)]
+        for c in range(cap):
+            mats_out[n * cap + c] = news[c]
+        return 0
+
+    lax.fori_loop(0, slots // cap, last_update, 0)
 
     col = err_col[pl.ds(pl.multiple_of(o * chunk, SUB), chunk), :]
     parts = chunk // SUB
@@ -569,6 +584,8 @@
     cap = slots // groups
     chunk = samples // owners
     devices = groups * owners
+    pad = jnp.zeros((2 * LANES - samples,), labels.dtype)
+    small = jnp.concatenate([labels, pad] + [x.reshape(-1) for x in (pair_first, pair_second, pair_count)])[None]
     smem = pl.BlockSpec(memory_space=pltpu.SMEM)
     vmem = pl.BlockSpec(memory_space=pltpu.VMEM)
     hbm = pl.BlockSpec(memory_space=pltpu.HBM)
@@ -581,7 +598,7 @@
             jax.ShapeDtypeStruct((chunk, per_block, feature), f32),
             jax.ShapeDtypeStruct((slots, feature, feature), f32),
         ),
-        in_specs=[smem] * 3 + [vmem] + [hbm] * 2,
+        in_specs=[smem, vmem, hbm, hbm],
         out_specs=(vmem,) * 3,
         scratch_shapes=[
             pltpu.SMEM((slots,), i32),
@@ -618,7 +635,7 @@
             collective_id=0, has_side_effects=True, vmem_limit_bytes=52 * 1024 * 1024
         ),
         cost_estimate=pl.CostEstimate(flops=4 * 10**9, bytes_accessed=8 * 10**6, transcendentals=400),
-    )(pair_first, pair_second, pair_count, labels.reshape(1, samples), fields, pair_mats[0, 0])
+    )(small, small, fields, pair_mats[0, 0])
     return (logits.reshape(samples), grad, new_mats[None, None])
 
 

time: 73.2 us -> 73.4 us (level)
  other arithmetic: 0 us -> 1.34 us
    unnamed x9 -> x4, local copies, waits for them, and re-layouts: 4.42 us -> 2.93 us
    unnamed x0 -> x1, other arithmetic: none -> 1.34 us
    concatenate x0 -> x1, local copies, waits for them, and re-layouts: none -> 0.76 us  [on_device_kernel(): jnp.concatenate([labels, pad] + [x.reshape(-1) for x in (pair_first, pair...]
where the time goes in v4:
time: 73.4 us; the launch traced here: 73.2 us
  Pallas kernels  66.8 us (91%)
  local copies, waits for them, and re-layouts  3.78 us (5%)
  other arithmetic  1.34 us (2%)
  between operations  1.29 us (2%)
    pallas_call x1, Pallas kernels, on_device_kernel(): pl.pallas_call(functools.partial(step_kernel, groups, owners), out_shape=...  66.8 us
    unnamed x4, local copies, waits for them, and re-layouts  2.93 us

profile of v4, /device:TPU:0, one launch (start us, length us, event | category | flops | bytes accessed | tf_op | source)
XLA Modules:
  0.0 73.2 jit_solution(9975166242206987124)
XLA Ops:
  1.3 0.5 broadcast.3
  1.8 1.3 %reduce.3 = s32[4,16]{1,0:T(4,128)S(1)} reduce(s32[4,1,16]{2,1,0:T(1,128)} %param.9, s32[]{:T(128)} %broadcast.3), dimensions={1}, to_apply=%param.9.reduce_sub_computation.3 | reduce | bytes 516 | tf_op args[3]
  3.1 0.1 reshape.19
  3.2 0.8 %concatenate.3 = s32[337]{0:T(512)S(1)} concatenate(s32[192]{0:T(256)} %param.7, s32[64]{0:T(128)S(1)} %broadcast_in_dim.9, s32[16]{0:T(128)} %bitcast.8, s32[64]{0:T(128)S(1)} %reshape.19, s32[1]{0:T(128)} %bitcast.5), dimensions={0} | concatenate | bytes 2696 | tf_op jit(solution)/shard_map/concatenate | solution.py:588
  4.0 66.8 %shard_map.85 = (f32[1,192]{1,0:T(1,128)S(1)}, f32[24,64,128]{2,1,0:T(8,128)S(1)}, f32[16,128,128]{2,1,0:T(8,128)S(1)}) custom-call(s32[1,337]{1,0:T(1,128)S(1)} %broadcast_in_dim.10.small.small_vec, s32[1,337]{1,0:T(1,128)S(1)} %broadcast_in_dim.10.small.small_vec, bf16[192,64,128]{2,1,0:T(8,128)(2,1)} %fields_in.1, f32[16,128,128]{2,1,0:T(8,128)} %bitcast.9), custom_call_target="tpu_custom_call" | custom-call | flops 4000000000 | bytes 8000000 | tf_op jit(solution)/shard_map/pallas_call | solution.py:594
  70.8 0.6 copy.13
  71.3 0.9 %copy.14 = f32[24,64,128]{2,1,0:T(8,128)} copy(f32[24,64,128]{2,1,0:T(8,128)S(1)} %get-tuple-element.13) | data formatting | bytes 1572864
  72.2 1.0 %copy.15 = f32[1,1,16,128,128]{4,3,2,1,0:T(8,128)} copy(f32[1,1,16,128,128]{4,3,2,1,0:T(8,128)S(1)} %bitcast.6) | data formatting | bytes 2097152
  (2 shorter events, 0.0 us)

commit v5 on v3

--- a/solution.py
+++ b/solution.py
@@ -119,8 +119,9 @@
     logits_out, grad_out, mats_out,
     slot_of, places, fields, mats,
     first_vec, first_t, served_vec, second_vec, mats_mid, total,
+    tab_out, tab_in, served_mate, mate_second, mate_first, mate_t, send_m, got_m, unit_m, got_unit_m,
     msg1, got1, msg2, got2, term_a, term_b, send_a, send_b, got_a, got_b, err_col, acc,
-    sem_f, sem_m, sem_v, sem_m1, sem_m2, sem_a, sem_b,
+    sem_f, sem_m, sem_v, sem_m1, sem_m2, sem_as, sem_ar, sem_bs, sem_br, sem_tab, sem_w, sem_mat,
 ):
     samples, per_block, feature = fields.shape
     shift = per_block.bit_length() - 1
@@ -133,6 +134,14 @@
     me = g * owners + o
     logit_scale = logit_gain / math.sqrt(devices * slots)
     rate = step_size * logit_scale / (samples * feature)
+    wing = owners // 2
+    mate = lax.rem(o + wing, owners)
+    side = lax.div(o, wing)
+    half = samples // 2
+    base = pl.multiple_of(side * half, 16)
+    row_id = lax.broadcasted_iota(jnp.int32, (SUB, LANES), 0)
+    lane_id = lax.broadcasted_iota(jnp.int32, (SUB, LANES), 1)
+    eye = lax.broadcasted_iota(jnp.int32, (LANES, LANES), 0) == lax.broadcasted_iota(jnp.int32, (LANES, LANES), 1)
     inv_root = 1.0 / math.sqrt(feature)
     extra = 2 * LANES - samples
 
@@ -158,12 +167,20 @@
 
     lax.fori_loop(1, devices, greet, 0)
 
-    def gather(spots):
-        wide = SUB * per_block
+    wide = SUB * per_block
+
+    def pick_scalars(spots):
         lanes = lax.broadcasted_iota(jnp.int32, (SUB, wide), 1)
         lanes = lanes - lax.broadcasted_iota(jnp.int32, (SUB, wide), 0) * per_block
-        pick = jnp.concatenate([jnp.where(lanes == f, 1.0, 0.0) for f in spots], axis=0).astype(jnp.bfloat16)
-
+        return jnp.concatenate([jnp.where(lanes == f, 1.0, 0.0) for f in spots], axis=0).astype(jnp.bfloat16)
+
+    def pick_row(row):
+        column = jnp.sum(jnp.where(eye, row, 0.0), axis=1, keepdims=True)
+        column = (column + 0.5).astype(jnp.int32)
+        lanes = lax.broadcasted_iota(jnp.int32, (LANES, wide), 1)
+        return jnp.where(lanes == column, 1.0, 0.0).astype(jnp.bfloat16)
+
+    def gather(pick):
         def rows(out, start, size):
             def part(i, _):
                 at = pl.multiple_of(start + i * 16, 16)
@@ -201,16 +218,6 @@
             ]
             seen = seen + hit.astype(jnp.int32)
         served += found
-    gather_served = gather(served)
-    for r in range(RUNS):
-        load_fields(r).wait()
-        gather_served(served_vec, r * run, run)
-        if r == 0:
-            pl.semaphore_wait(barrier, devices - 1)
-        for j in range(1, groups):
-            vec_copy(j, r).start()
-    second_vec[pl.ds(g * cap, cap)] = served_vec[pl.ds(g * cap, cap)]
-
     owner_of = [jnp.int32(0)] * slots
     seen = [jnp.int32(0)] * groups
     for s in range(slots):
@@ -230,31 +237,91 @@
     def live_of(p):
         return jnp.where(slot_of[p] < count[0, 0], 1.0, 0.0)
 
-    gather(first_at)(first_vec, 0, samples)
-
-    def turn(p, _):
-        v = first_vec[p].astype(jnp.float32)
-        v = jnp.concatenate([v, jnp.zeros((extra, feature), jnp.float32)], axis=0)
-        first_t[p] = v.T.astype(jnp.bfloat16)
+    gather_served = gather(pick_scalars(served))
+    for r in range(RUNS):
+        load_fields(r).wait()
+        gather_served(served_vec, r * run, run)
+        if r == 0:
+            pl.semaphore_wait(barrier, devices - 1)
+        for j in range(1, groups):
+            vec_copy(j, r).start()
+    second_vec[pl.ds(g * cap, cap)] = served_vec[pl.ds(g * cap, cap)]
+
+    def full_row(ids):
+        spots = jnp.zeros((SUB, LANES), jnp.int32)
+        for t in range(slots):
+            spots = jnp.where(lane_id // SUB == t, ids[t], spots)
+        return (spots + (lane_id % SUB) * per_block).astype(jnp.float32)
+
+    tab_out[0:SUB, :] = jnp.where(row_id == 0, full_row(first_at), jnp.where(row_id == 1, full_row(served), 0.0))
+    for p in range(slots):
+        tab_out[SUB + p : SUB + p + 1, :] = jnp.zeros((1, LANES), jnp.float32) + live_of(p)
+
+    def to_mate(src, dst, sems, at):
+        return pltpu.make_async_remote_copy(
+            src_ref=src, dst_ref=dst, send_sem=sems.at[0, at], recv_sem=sems.at[1, at],
+            device_id=(g, mate), device_id_type=MESH,
+        )
+
+    tab_copy = to_mate(tab_out, tab_in, sem_tab, 0)
+    tab_copy.start()
+    load_mats.wait()
+
+    def code_mats(t, _):
+        a, b = mats[slot_of[2 * t]], mats[slot_of[2 * t + 1]]
+        big = jnp.maximum(jnp.max(jnp.maximum(jnp.abs(a), jnp.abs(b)), axis=0, keepdims=True), 1e-30)
+        gain = TOP / big
+        a, b = [jnp.floor(x * gain + 0.5).astype(jnp.int32) for x in (a, b)]
+        send_m[t] = (a & 0xFFFF) | (b << 16)
+        unit_m[pl.ds(t, 1), :] = big * (1.0 / TOP)
         return 0
 
-    lax.fori_loop(0, slots, turn, 0)
+    lax.fori_loop(0, slots // 2, code_mats, 0)
+    part = slots // 4
+    mat_copies = [to_mate(send_m.at[pl.ds(h * part, part)], got_m.at[pl.ds(h * part, part)], sem_mat, h) for h in range(2)]
+    mat_copies.append(to_mate(unit_m, got_unit_m, sem_mat, 2))
+    mat_copies[2].start()
+    mat_copies[0].start()
+
+    tab_copy.wait_recv()
+    gather(pick_row(tab_in[1:2, :]))(served_mate, 0, samples)
+
+    def mate_copy(j):
+        to = lax.rem(g + j, groups)
+        return pltpu.make_async_remote_copy(
+            src_ref=served_mate.at[pl.ds(to * cap, cap)], dst_ref=mate_second.at[pl.ds(g * cap, cap)],
+            send_sem=sem_w.at[0, j], recv_sem=sem_w.at[1, j], device_id=(to, o), device_id_type=MESH,
+        )
+
+    for j in range(1, groups):
+        mate_copy(j).start()
+    mate_second[pl.ds(g * cap, cap)] = served_mate[pl.ds(g * cap, cap)]
+    gather(pick_scalars(first_at))(first_vec, 0, samples)
+
+    def turn_all(vecs, turned):
+        def turn(p, _):
+            v = vecs[p].astype(jnp.float32)
+            v = jnp.concatenate([v, jnp.zeros((extra, feature), jnp.float32)], axis=0)
+            turned[p] = v.T.astype(jnp.bfloat16)
+            return 0
+
+        lax.fori_loop(0, slots, turn, 0)
+
+    turn_all(first_vec, first_t)
     total[...] = jnp.zeros_like(total)
 
-    def mix(p, mat):
-        v1 = first_vec[p]
-        high, low = two_parts(mat)
-        return dot32(jnp.concatenate([v1, v1], axis=1), jnp.concatenate([high, low], axis=0)), high, low
-
     def first_pass(q):
+        spots = [q * cap + c for c in range(cap)]
+        split = [two_parts(mats[slot_of[p]]) for p in spots]
+        firsts = [first_vec[p] for p in spots]
+        mixed = [
+            dot32(jnp.concatenate([v, v], axis=1), jnp.concatenate(parts, axis=0)) for v, parts in zip(firsts, split)
+        ]
         sums = total[...]
-        for c in range(cap):
-            p = q * cap + c
-            mixed, _, _ = mix(p, mats[slot_of[p]])
-            sums = sums + (mixed * second_vec[p].astype(jnp.float32)) * live_of(p)
+        for m, p in zip(mixed, spots):
+            sums = sums + (m * second_vec[p].astype(jnp.float32)) * live_of(p)
         total[...] = sums
 
-    load_mats.wait()
     first_pass(g)
     for j in range(1, groups):
         for r in range(RUNS):
@@ -269,8 +336,6 @@
             for t in (total[0:LANES], tail)
         ]
 
-    row_id = lax.broadcasted_iota(jnp.int32, (SUB, LANES), 0)
-    lane_id = lax.broadcasted_iota(jnp.int32, (SUB, LANES), 1)
     segment = cap * SUB
     span = LANES // segment
 
@@ -293,7 +358,7 @@
         peer = lax.rem(me + d, devices)
         pg, po = lax.div(peer, owners), lax.rem(peer, owners)
         return pltpu.make_async_remote_copy(
-            src_ref=src.at[po if pick_own else pg],
+            src_ref=src.at[lax.rem(po, wing) if pick_own else pg],
             dst_ref=dst.at[me],
             send_sem=sems.at[0, peer],
             recv_sem=sems.at[1, me],
@@ -346,13 +411,14 @@
     def error_row(err):
         return jnp.concatenate([err[0:1], err[1:2, 0 : samples - LANES]], axis=1)
 
-    def gradient(p, erow):
-        v = first_t[p][:, 0:samples].astype(jnp.float32) * erow
-        high, low = two_parts(v)
-        v2 = second_vec[p]
-        return dot32(high, v2) + dot32(low, v2)
+    def gradients(spots, erow, turned_ref, second_ref):
+        turned = [turned_ref[p][:, 0:samples].astype(jnp.float32) * erow for p in spots]
+        both = [jnp.concatenate(two_parts(v), axis=0) for v in turned]
+        out = [dot32(v, second_ref[p]) for v, p in zip(both, spots)]
+        return [x[0:feature] + x[feature:] for x in out]
 
     send_tiles(msg1, got1, sem_m1, False)
+    mat_copies[1].start()
     got1[me] = msg1[g]
     wait_tiles(msg1, got1, sem_m1)
     _, err = errors_of(got1, 0)
@@ -360,30 +426,53 @@
     total[...] = jnp.zeros_like(total)
     msg2[...] = jnp.zeros_like(msg2)
 
-    def second_pass(j):
-        q = lax.rem(g + j, groups)
-        sums = total[...]
-        for c in range(cap):
-            p = q * cap + c
-            live = live_of(p)
-            mid = mats[slot_of[p]] - (rate * live) * gradient(p, erow)
-            mats_mid[p] = mid
-            mixed, high, low = mix(p, mid)
-            v2 = second_vec[p]
-            first = lax.dot_general(
-                jnp.concatenate([v2, v2], axis=1),
-                jnp.concatenate([high, low], axis=1),
-                NT,
-                preferred_element_type=jnp.float32,
-            )
-            sums = sums + (mixed * v2.astype(jnp.float32)) * live
-            factor = live * inv_root
-            term_a[c] = first * factor
-            term_b[c] = mixed * factor
-        total[...] = sums
+    def halved(ref, p):
+        return ref[p, pl.ds(base, half), :]
+
+    def twice(v):
+        return jnp.concatenate([v, v], axis=1)
+
+    def second_pass(q, m):
+        spots = [q * cap + c for c in range(cap)]
+        if m == 0:
+            lives = [live_of(p) for p in spots]
+            old = [mats[slot_of[p]] for p in spots]
+            firsts = [first_vec[p] for p in spots]
+            seconds = [halved(second_vec, p) for p in spots]
+            moves = gradients(spots, erow, first_t, second_vec)
+        else:
+            lives = [tab_in[pl.ds(SUB + p, 1), :] for p in spots]
+            old = []
+            for k in range(pairs):
+                w = got_m[q * pairs + k]
+                unit = got_unit_m[pl.ds(q * pairs + k, 1), :]
+                old += [((w << 16) >> 16).astype(jnp.float32) * unit, (w >> 16).astype(jnp.float32) * unit]
+            firsts = [halved(mate_first, p) for p in spots]
+            seconds = [halved(mate_second, p) for p in spots]
+            moves = gradients(spots, erow, mate_t, mate_second)
+        mids = [x - (rate * live) * d for x, d, live in zip(old, moves, lives)]
+        split = [two_parts(x) for x in mids]
+        mixed = [dot32(twice(v), jnp.concatenate(parts, axis=0)) for v, parts in zip(firsts, split)]
+        back = [
+            lax.dot_general(twice(v), jnp.concatenate(parts, axis=1), NT, preferred_element_type=jnp.float32)
+            for v, parts in zip(seconds, split)
+        ]
+        if m == 0:
+            sums = total[...]
+            for x, p, live in zip(mixed, spots, lives):
+                sums = sums + (x * second_vec[p].astype(jnp.float32)) * live
+            total[...] = sums
+        for c, p in enumerate(spots):
+            factor = lives[c] * inv_root
+            term_a[c, pl.ds(base, half), :] = back[c] * factor
+            if m == 0:
+                mats_mid[p] = mids[c]
+                term_b[c] = mixed[c] * factor
+            else:
+                term_b[c, pl.ds(base, half), :] = mixed[c] * factor
 
         def code(w, _):
-            rows = pl.ds(pl.multiple_of(w * chunk, SUB), chunk)
+            rows = pl.ds(pl.multiple_of(base + w * chunk, SUB), chunk)
             terms = [t[c, rows, :] for t in (term_a, term_b) for c in range(cap)]
             big = functools.reduce(jnp.maximum, [jnp.abs(t) for t in terms])
             big = jnp.maximum(jnp.max(big, axis=0, keepdims=True), 1e-30)
@@ -392,11 +481,11 @@
             for at, out in ((0, send_a), (cap, send_b)):
                 for k in range(pairs):
                     a, b = whole[at + 2 * k], whole[at + 2 * k + 1]
-                    out[q, w, pl.ds(k * chunk, chunk), :] = (a & 0xFFFF) | (b << 16)
-            msg2[w, pl.ds(q, 1), :] = big * (1.0 / TOP)
+                    out[m, q, w, pl.ds(k * chunk, chunk), :] = (a & 0xFFFF) | (b << 16)
+            msg2[w, pl.ds(m * SUB + q, 1), :] = big * (1.0 / TOP)
             return 0
 
-        lax.fori_loop(0, owners, code, 0)
+        lax.fori_loop(0, wing, code, 0)
 
     def partner(k):
         w, bit = o, 1
@@ -405,65 +494,81 @@
             bit *= 2
         return w
 
-    order = [k for pair in zip(range(owners // 2, owners), [*range(1, owners // 2), 0]) for k in pair if k]
-
-    def unit_a(j, k):
-        q, w = lax.rem(g + j, groups), partner(k)
+    mine = o - side * wing
+
+    def unit_a(m, q, k):
+        w = partner(k)
         return pltpu.make_async_remote_copy(
-            src_ref=send_a.at[q, w], dst_ref=got_a.at[o, q], send_sem=sem_a.at[0, q, w],
-            recv_sem=sem_a.at[1, q, o], device_id=(g, w), device_id_type=MESH,
-        )
-
-    def unit_b(j, k):
-        q, w = lax.rem(g + j, groups), partner(k)
+            src_ref=send_a.at[m, q, w - side * wing], dst_ref=got_a.at[mate if m else o, q],
+            send_sem=sem_as.at[m, q, k], recv_sem=sem_ar.at[q, mate if m else o],
+            device_id=(g, w), device_id_type=MESH,
+        )
+
+    def unit_b(m, q, k):
+        w = partner(k)
         return pltpu.make_async_remote_copy(
-            src_ref=send_b.at[q, w], dst_ref=got_b.at[g, o], send_sem=sem_b.at[0, q, w],
-            recv_sem=sem_b.at[1, g, o], device_id=(q, w), device_id_type=MESH,
-        )
-
-    def send_units(j):
-        for k in order:
-            unit_a(j, k).start()
-            unit_b(j, k).start()
+            src_ref=send_b.at[m, q, w - side * wing], dst_ref=got_b.at[g, mate if m else o],
+            send_sem=sem_bs.at[m, q, k], recv_sem=sem_br.at[g, mate if m else o],
+            device_id=(q, w), device_id_type=MESH,
+        )
+
+    def send_units(q, m):
+        for k in range(1, wing):
+            unit_a(m, q, k).start()
+            unit_b(m, q, k).start()
+        got_a[mate if m else o, q] = send_a[m, q, mine]
+
+        @pl.when(q == g)
+        def _():
+            got_b[g, mate if m else o] = send_b[m, g, mine]
+
+        @pl.when(q != g)
+        def _():
+            unit_b(m, q, 0).start()
+
+    def own_part(j, _):
         q = lax.rem(g + j, groups)
-        got_a[o, q] = send_a[q, o]
-
-    second_pass(0)
-    got_b[g, o] = send_b[g, o]
-    send_units(0)
-
-    def later(j, _):
-        second_pass(j)
+        second_pass(q, 0)
+        send_units(q, 0)
         return 0
 
-    lax.fori_loop(1, groups, later, 0)
+    lax.fori_loop(0, groups, own_part, 0)
     r0, r1 = partial_rows()
-    for w in range(owners):
-        msg2[w] = jnp.where(row_id == groups, r0, jnp.where(row_id == groups + 1, r1, msg2[w]))
+    gather(pick_row(tab_in[0:1, :]))(mate_first, 0, samples)
+    turn_all(mate_first, mate_t)
+    for j in range(1, groups):
+        mate_copy(j).wait_recv()
+    for copy in mat_copies:
+        copy.wait_recv()
+
+    def mate_part(q, _):
+        second_pass(q, 1)
+        send_units(q, 1)
+        return 0
+
+    lax.fori_loop(0, groups, mate_part, 0)
+    for w in range(wing):
+        low = msg2[w, 0:SUB, :]
+        msg2[w, 0:SUB, :] = jnp.where(row_id == groups, r0, jnp.where(row_id == groups + 1, r1, low))
     send_tiles(msg2, got2, sem_m2, True)
-
-    def send_later(j, _):
-        unit_b(j, 0).start()
-        send_units(j)
-        return 0
-
-    lax.fori_loop(1, groups, send_later, 0)
-    got2[me] = msg2[o]
+    got2[me] = msg2[mine]
     wait_tiles(msg2, got2, sem_m2)
     logits, err = errors_of(got2, groups)
     logits_out[...] = error_row(logits)
     erow = error_row(err)
-    eye = lax.broadcasted_iota(jnp.int32, (LANES, LANES), 0) == lax.broadcasted_iota(jnp.int32, (LANES, LANES), 1)
-    for half in range(2):
-        column = jnp.sum(jnp.where(eye, err[half : half + 1], 0.0), axis=1, keepdims=True)
-        err_col[pl.ds(half * LANES, LANES), :] = jnp.broadcast_to(column, (LANES, LANES))
-
-    def last_update(s, _):
-        p = places[s]
-        mats_out[s] = mats_mid[p] - (rate * live_of(p)) * gradient(p, erow)
+    for n in range(2):
+        column = jnp.sum(jnp.where(eye, err[n : n + 1], 0.0), axis=1, keepdims=True)
+        err_col[pl.ds(n * LANES, LANES), :] = jnp.broadcast_to(column, (LANES, LANES))
+
+    def last_update(n, _):
+        spots = [places[n * cap + c] for c in range(cap)]
+        moves = gradients(spots, erow, first_t, second_vec)
+        news = [mats_mid[p] - (rate * live_of(p)) * d for p, d in zip(spots, moves)]
+        for c in range(cap):
+            mats_out[n * cap + c] = news[c]
         return 0
 
-    lax.fori_loop(0, slots, last_update, 0)
+    lax.fori_loop(0, slots // cap, last_update, 0)
 
     col = err_col[pl.ds(pl.multiple_of(o * chunk, SUB), chunk), :]
     parts = chunk // SUB
@@ -491,38 +596,40 @@
 
     def wait_a(q, w):
         pltpu.make_async_remote_copy(
-            src_ref=send_a.at[q, w], dst_ref=got_a.at[w, q], send_sem=sem_a.at[0, q, w],
-            recv_sem=sem_a.at[1, q, w], device_id=(g, w), device_id_type=MESH,
+            src_ref=send_a.at[0, q, 0], dst_ref=got_a.at[w, q], send_sem=sem_as.at[0, q, 0],
+            recv_sem=sem_ar.at[q, w], device_id=(g, w), device_id_type=MESH,
         ).wait_recv()
 
     def wait_b(q, w):
         pltpu.make_async_remote_copy(
-            src_ref=send_b.at[q, w], dst_ref=got_b.at[q, w], send_sem=sem_b.at[0, q, w],
-            recv_sem=sem_b.at[1, q, w], device_id=(q, w), device_id_type=MESH,
+            src_ref=send_b.at[0, q, 0], dst_ref=got_b.at[q, w], send_sem=sem_bs.at[0, q, 0],
+            recv_sem=sem_br.at[q, w], device_id=(q, w), device_id_type=MESH,
         ).wait_recv()
 
     acc[...] = jnp.zeros_like(acc)
 
     def arrivals(n, _):
-        j, h = n // (owners // span), n % (owners // span)
+        j, h = n % groups, n // groups
         qa, qb = lax.rem(g + j, groups), lax.rem(g + groups - j, groups)
         terms_a, terms_b, spots_a, spots_b = [], [], 0.0, 0.0
         for i in range(span):
             k = h * span + partner(i) % span
             w = partner(k)
-
-            @pl.when(k > 0)
+            near = k % wing
+            real = partner(near)
+
+            @pl.when(near > 0)
             def _():
                 wait_a(qa, w)
 
-            @pl.when(j + k > 0)
+            @pl.when(j + near > 0)
             def _():
                 wait_b(qb, w)
 
-            scale = got2[g * owners + w, pl.ds(qa, 1), :]
+            scale = got2[g * owners + real, pl.ds(h * SUB + qa, 1), :]
             terms_a += decode(lambda m: got_a[w, qa, pl.ds(m * chunk, chunk), :], scale)
             spots_a = spots_a + got1[g * owners + w, pl.ds(FIRST_ROW + qa, 1), :]
-            scale = got2[qb * owners + w, pl.ds(g, 1), :]
+            scale = got2[qb * owners + real, pl.ds(h * SUB + g, 1), :]
             terms_b += decode(lambda m: got_b[qb, w, pl.ds(m * chunk, chunk), :], scale)
             spots_b = spots_b + got1[qb * owners + w][SECOND_ROW : SECOND_ROW + 1]
         pick = jnp.concatenate(pick_of(spots_a) + pick_of(spots_b), axis=1)
@@ -544,17 +651,20 @@
 
     lax.fori_loop(1, devices, drain_tiles, 0)
 
-    def drain_units(j, _):
-        def one(k, _):
-            unit_a(j, k).wait_send()
-            unit_b(j, k).wait_send()
-            return 0
-
-        lax.fori_loop(1, owners, one, 0)
-
-        @pl.when(j > 0)
-        def _():
-            unit_b(j, 0).wait_send()
+    for j in range(1, groups):
+        mate_copy(j).wait_send()
+    for copy in mat_copies + [tab_copy]:
+        copy.wait_send()
+
+    def drain_units(q, _):
+        for m in range(2):
+            for k in range(1, wing):
+                unit_a(m, q, k).wait_send()
+                unit_b(m, q, k).wait_send()
+
+            @pl.when(q != g)
+            def _():
+                unit_b(m, q, 0).wait_send()
 
         return 0
 
@@ -594,14 +704,24 @@
             pltpu.VMEM((slots, samples, feature), bf16),
             pltpu.VMEM((slots, feature, feature), f32),
             pltpu.VMEM((samples, feature), f32),
+            pltpu.VMEM((SUB + slots, LANES), f32),
+            pltpu.VMEM((SUB + slots, LANES), f32),
+            pltpu.VMEM((slots, samples, feature), bf16),
+            pltpu.VMEM((slots, samples, feature), bf16),
+            pltpu.VMEM((slots, samples, feature), bf16),
+            pltpu.VMEM((slots, feature, 2 * LANES), bf16),
+            pltpu.VMEM((slots // 2, feature, feature), i32),
+            pltpu.VMEM((slots // 2, feature, feature), i32),
+            pltpu.VMEM((slots // 2, feature), f32),
+            pltpu.VMEM((slots // 2, feature), f32),
             pltpu.VMEM((groups, SUB, LANES), f32),
             pltpu.VMEM((devices, SUB, LANES), f32),
-            pltpu.VMEM((owners, SUB, LANES), f32),
-            pltpu.VMEM((devices, SUB, LANES), f32),
+            pltpu.VMEM((owners // 2, 2 * SUB, LANES), f32),
+            pltpu.VMEM((devices, 2 * SUB, LANES), f32),
             pltpu.VMEM((cap, samples, feature), f32),
             pltpu.VMEM((cap, samples, feature), f32),
-            pltpu.VMEM((groups, owners, rows, feature), i32),
-            pltpu.VMEM((groups, owners, rows, feature), i32),
+            pltpu.VMEM((2, groups, owners // 2, rows, feature), i32),
+            pltpu.VMEM((2, groups, owners // 2, rows, feature), i32),
             pltpu.VMEM((owners, groups, rows, feature), i32),
             pltpu.VMEM((groups, owners, rows, feature), i32),
             pltpu.VMEM((2 * LANES, LANES), f32),
@@ -611,8 +731,13 @@
             pltpu.SemaphoreType.DMA((2, groups, RUNS)),
             pltpu.SemaphoreType.DMA((2, devices)),
             pltpu.SemaphoreType.DMA((2, devices)),
-            pltpu.SemaphoreType.DMA((2, groups, owners)),
-            pltpu.SemaphoreType.DMA((2, groups, owners)),
+            pltpu.SemaphoreType.DMA((2, groups, owners // 2)),
+            pltpu.SemaphoreType.DMA((groups, owners)),
+            pltpu.SemaphoreType.DMA((2, groups, owners // 2)),
+            pltpu.SemaphoreType.DMA((groups, owners)),
+            pltpu.SemaphoreType.DMA((2, 1)),
+            pltpu.SemaphoreType.DMA((2, groups)),
+            pltpu.SemaphoreType.DMA((2, 3)),
         ],
         compiler_params=pltpu.CompilerParams(
             collective_id=0, has_side_effects=True, vmem_limit_bytes=52 * 1024 * 1024
@@ -636,7 +761,8 @@
         and samples % (16 * RUNS) == 0
         and fields.shape[1] & (fields.shape[1] - 1) == 0
         and owners & (owners - 1) == 0
-        and owners % (LANES // (cap * SUB)) == 0
+        and owners == 2 * (LANES // (cap * SUB))
+        and samples % 32 == 0
         and FIRST_ROW + groups <= SUB
     )
 

time: 73.2 us -> 75.6 us (1.033)
  Pallas kernels: 67.3 us -> 69.6 us
    pallas_call x1, Pallas kernels: 67.3 us -> 69.6 us  [on_device_kernel(): pl.pallas_call(functools.partial(step_kernel, groups, owners), out_shape=...]
where the time goes in v5:
time: 75.6 us; the launch traced here: 75.3 us
  Pallas kernels  69.6 us (92%)
  local copies, waits for them, and re-layouts  4.42 us (6%)
  between operations  1.3 us (2%)
    pallas_call x1, Pallas kernels, on_device_kernel(): pl.pallas_call(functools.partial(step_kernel, groups, owners), out_shape=...  69.6 us
    unnamed x9, local copies, waits for them, and re-layouts  4.42 us

profile of v5, /device:TPU:0, one launch (start us, length us, event | category | flops | bytes accessed | tf_op | source)
XLA Modules:
  0.0 75.3 jit_solution(8515758948856442963)
XLA Ops:
  1.3 0.0 copy-start
  1.3 0.7 copy-done
  2.0 0.0 copy-start.1
  2.0 0.7 copy-done.1
  2.6 0.0 copy-start.2
  2.6 0.7 copy-done.2
  3.3 69.6 %shard_map.85 = (f32[1,192]{1,0:T(1,128)S(1)}, f32[24,64,128]{2,1,0:T(8,128)S(1)}, f32[16,128,128]{2,1,0:T(8,128)S(1)}) custom-call(s32[1,1,16]{2,1,0:T(1,128)S(1)} %copy-done.2, s32[4,1,16]{2,1,0:T(1,128)S(1)} %copy-done, s32[1,1]{1,0:T(1,128)S(6)} %copy.12.count, s32[1,192]{1,0:T(1,128)S(1)} %bitcast.6, bf16[192,64,128]{2,1,0:T(8,128)(2,1)} %fields_in.1, ...), custom_call_target="tpu_custom_call" | custom-call | flops 4000000000 | bytes 8000000 | tf_op jit(solution)/shard_map/pallas_call | solution.py:687
  72.9 0.6 copy.13
  73.5 0.9 %copy.14 = f32[24,64,128]{2,1,0:T(8,128)} copy(f32[24,64,128]{2,1,0:T(8,128)S(1)} %get-tuple-element.13) | data formatting | bytes 1572864
  74.4 1.0 %copy.15 = f32[1,1,16,128,128]{4,3,2,1,0:T(8,128)} copy(f32[1,1,16,128,128]{4,3,2,1,0:T(8,128)S(1)} %bitcast.4) | data formatting | bytes 2097152
Async XLA Ops:
  1.3 0.7 copy-start
  2.0 0.7 copy-start.1
  2.6 0.7 copy-start.2

commit v6 on v5

--- a/solution.py
+++ b/solution.py
@@ -120,8 +120,8 @@
     slot_of, places, fields, mats,
     first_vec, first_t, served_vec, second_vec, mats_mid, total,
     tab_out, tab_in, served_mate, mate_second, mate_first, mate_t, send_m, got_m, unit_m, got_unit_m,
-    msg1, got1, msg2, got2, term_a, term_b, send_a, send_b, got_a, got_b, err_col, acc,
-    sem_f, sem_m, sem_v, sem_m1, sem_m2, sem_as, sem_ar, sem_bs, sem_br, sem_tab, sem_w, sem_mat,
+    msg1, got1, msg2, got2, msg3, got3, term_a, term_b, send_a, send_b, got_a, got_b, err_col, acc,
+    sem_f, sem_m, sem_v, sem_m1, sem_m2, sem_m3, sem_as, sem_ar, sem_bs, sem_br, sem_tab, sem_w, sem_mat,
 ):
     samples, per_block, feature = fields.shape
     shift = per_block.bit_length() - 1
@@ -184,14 +184,13 @@
         def rows(out, start, size):
             def part(i, _):
                 at = pl.multiple_of(start + i * 16, 16)
-                halves = []
-                for h in range(2):
-                    block = fields[pl.ds(at + h * SUB, SUB)].reshape(wide, feature)
-                    halves.append(dot32(pick, block).reshape(slots, SUB, feature))
+                blocks = [fields[pl.ds(at + h * SUB, SUB)].reshape(wide, feature) for h in range(2)]
+                both = dot32(pick, jnp.concatenate(blocks, axis=1))
+                halves = [both[:, h * feature : (h + 1) * feature].reshape(slots, SUB, feature) for h in range(2)]
                 out[:, pl.ds(at, 16), :] = jnp.concatenate(halves, axis=1).astype(jnp.bfloat16)
                 return 0
 
-            lax.fori_loop(0, size // 16, part, 0)
+            lax.fori_loop(0, size // 16, part, 0, unroll=3)
 
         return rows
 
@@ -276,26 +275,12 @@
         unit_m[pl.ds(t, 1), :] = big * (1.0 / TOP)
         return 0
 
-    lax.fori_loop(0, slots // 2, code_mats, 0)
+    lax.fori_loop(0, slots // 4, code_mats, 0, unroll=2)
     part = slots // 4
     mat_copies = [to_mate(send_m.at[pl.ds(h * part, part)], got_m.at[pl.ds(h * part, part)], sem_mat, h) for h in range(2)]
     mat_copies.append(to_mate(unit_m, got_unit_m, sem_mat, 2))
-    mat_copies[2].start()
     mat_copies[0].start()
 
-    tab_copy.wait_recv()
-    gather(pick_row(tab_in[1:2, :]))(served_mate, 0, samples)
-
-    def mate_copy(j):
-        to = lax.rem(g + j, groups)
-        return pltpu.make_async_remote_copy(
-            src_ref=served_mate.at[pl.ds(to * cap, cap)], dst_ref=mate_second.at[pl.ds(g * cap, cap)],
-            send_sem=sem_w.at[0, j], recv_sem=sem_w.at[1, j], device_id=(to, o), device_id_type=MESH,
-        )
-
-    for j in range(1, groups):
-        mate_copy(j).start()
-    mate_second[pl.ds(g * cap, cap)] = served_mate[pl.ds(g * cap, cap)]
     gather(pick_scalars(first_at))(first_vec, 0, samples)
 
     def turn_all(vecs, turned):
@@ -305,8 +290,9 @@
             turned[p] = v.T.astype(jnp.bfloat16)
             return 0
 
-        lax.fori_loop(0, slots, turn, 0)
-
+        lax.fori_loop(0, slots, turn, 0, unroll=4)
+
+    lax.fori_loop(slots // 4, slots // 2, code_mats, 0, unroll=2)
     turn_all(first_vec, first_t)
     total[...] = jnp.zeros_like(total)
 
@@ -418,13 +404,28 @@
         return [x[0:feature] + x[feature:] for x in out]
 
     send_tiles(msg1, got1, sem_m1, False)
+    mat_copies[2].start()
     mat_copies[1].start()
+    tab_copy.wait_recv()
+    gather(pick_row(tab_in[1:2, :]))(served_mate, 0, samples)
+
+    def mate_copy(j):
+        to = lax.rem(g + j, groups)
+        return pltpu.make_async_remote_copy(
+            src_ref=served_mate.at[pl.ds(to * cap, cap)], dst_ref=mate_second.at[pl.ds(g * cap, cap)],
+            send_sem=sem_w.at[0, j], recv_sem=sem_w.at[1, j], device_id=(to, o), device_id_type=MESH,
+        )
+
+    for j in range(1, groups):
+        mate_copy(j).start()
+    mate_second[pl.ds(g * cap, cap)] = served_mate[pl.ds(g * cap, cap)]
     got1[me] = msg1[g]
     wait_tiles(msg1, got1, sem_m1)
     _, err = errors_of(got1, 0)
     erow = error_row(err)
     total[...] = jnp.zeros_like(total)
     msg2[...] = jnp.zeros_like(msg2)
+    msg3[...] = jnp.zeros_like(msg3)
 
     def halved(ref, p):
         return ref[p, pl.ds(base, half), :]
@@ -482,7 +483,7 @@
                 for k in range(pairs):
                     a, b = whole[at + 2 * k], whole[at + 2 * k + 1]
                     out[m, q, w, pl.ds(k * chunk, chunk), :] = (a & 0xFFFF) | (b << 16)
-            msg2[w, pl.ds(m * SUB + q, 1), :] = big * (1.0 / TOP)
+            (msg3 if m else msg2)[w, pl.ds(q, 1), :] = big * (1.0 / TOP)
             return 0
 
         lax.fori_loop(0, wing, code, 0)
@@ -534,6 +535,9 @@
 
     lax.fori_loop(0, groups, own_part, 0)
     r0, r1 = partial_rows()
+    for w in range(wing):
+        msg2[w] = jnp.where(row_id == groups, r0, jnp.where(row_id == groups + 1, r1, msg2[w]))
+    send_tiles(msg2, got2, sem_m2, True)
     gather(pick_row(tab_in[0:1, :]))(mate_first, 0, samples)
     turn_all(mate_first, mate_t)
     for j in range(1, groups):
@@ -547,10 +551,26 @@
         return 0
 
     lax.fori_loop(0, groups, mate_part, 0)
-    for w in range(wing):
-        low = msg2[w, 0:SUB, :]
-        msg2[w, 0:SUB, :] = jnp.where(row_id == groups, r0, jnp.where(row_id == groups + 1, r1, low))
-    send_tiles(msg2, got2, sem_m2, True)
+    def scale_copy(n, k):
+        gg, w = lax.rem(g + n, groups), partner(k)
+        return pltpu.make_async_remote_copy(
+            src_ref=msg3.at[w - side * wing], dst_ref=got3.at[me],
+            send_sem=sem_m3.at[0, gg * owners + w], recv_sem=sem_m3.at[1, me],
+            device_id=(gg, w), device_id_type=MESH,
+        )
+
+    def scale_arrival(n, k):
+        gg, w = lax.rem(g + n, groups), partner(k)
+        src = gg * owners + w
+        return pltpu.make_async_remote_copy(
+            src_ref=msg3.at[0], dst_ref=got3.at[src], send_sem=sem_m3.at[0, src], recv_sem=sem_m3.at[1, src],
+            device_id=(gg, w), device_id_type=MESH,
+        )
+
+    near_peers = [(n, k) for n in range(groups) for k in range(wing) if n + k]
+    for n, k in near_peers:
+        scale_copy(n, k).start()
+    got3[me] = msg3[mine]
     got2[me] = msg2[mine]
     wait_tiles(msg2, got2, sem_m2)
     logits, err = errors_of(got2, groups)
@@ -607,6 +627,13 @@
         ).wait_recv()
 
     acc[...] = jnp.zeros_like(acc)
+
+    for n, k in near_peers:
+        scale_arrival(n, k).wait_recv()
+
+    def scale_row(h, src, row):
+        rows = pl.ds(row, 1)
+        return jnp.where(h == 0, got2[src, rows, :], got3[src, rows, :])
 
     def arrivals(n, _):
         j, h = n % groups, n // groups
@@ -626,10 +653,10 @@
             def _():
                 wait_b(qb, w)
 
-            scale = got2[g * owners + real, pl.ds(h * SUB + qa, 1), :]
+            scale = scale_row(h, g * owners + real, qa)
             terms_a += decode(lambda m: got_a[w, qa, pl.ds(m * chunk, chunk), :], scale)
             spots_a = spots_a + got1[g * owners + w, pl.ds(FIRST_ROW + qa, 1), :]
-            scale = got2[qb * owners + real, pl.ds(h * SUB + g, 1), :]
+            scale = scale_row(h, qb * owners + real, g)
             terms_b += decode(lambda m: got_b[qb, w, pl.ds(m * chunk, chunk), :], scale)
             spots_b = spots_b + got1[qb * owners + w][SECOND_ROW : SECOND_ROW + 1]
         pick = jnp.concatenate(pick_of(spots_a) + pick_of(spots_b), axis=1)
@@ -655,6 +682,8 @@
         mate_copy(j).wait_send()
     for copy in mat_copies + [tab_copy]:
         copy.wait_send()
+    for n, k in near_peers:
+        scale_copy(n, k).wait_send()
 
     def drain_units(q, _):
         for m in range(2):
@@ -716,8 +745,10 @@
             pltpu.VMEM((slots // 2, feature), f32),
             pltpu.VMEM((groups, SUB, LANES), f32),
             pltpu.VMEM((devices, SUB, LANES), f32),
-            pltpu.VMEM((owners // 2, 2 * SUB, LANES), f32),
-            pltpu.VMEM((devices, 2 * SUB, LANES), f32),
+            pltpu.VMEM((owners // 2, SUB, LANES), f32),
+            pltpu.VMEM((devices, SUB, LANES), f32),
+            pltpu.VMEM((owners // 2, SUB, LANES), f32),
+            pltpu.VMEM((devices, SUB, LANES), f32),
             pltpu.VMEM((cap, samples, feature), f32),
             pltpu.VMEM((cap, samples, feature), f32),
             pltpu.VMEM((2, groups, owners // 2, rows, feature), i32),
@@ -729,6 +760,7 @@
             pltpu.SemaphoreType.DMA((RUNS,)),
             pltpu.SemaphoreType.DMA((1,)),
             pltpu.SemaphoreType.DMA((2, groups, RUNS)),
+            pltpu.SemaphoreType.DMA((2, devices)),
             pltpu.SemaphoreType.DMA((2, devices)),
             pltpu.SemaphoreType.DMA((2, devices)),
             pltpu.SemaphoreType.DMA((2, groups, owners // 2)),

time: 75.6 us -> 71.8 us (0.950)
  Pallas kernels: 69.6 us -> 65.9 us
    pallas_call x1, Pallas kernels: 69.6 us -> 65.9 us  [on_device_kernel(): pl.pallas_call(functools.partial(step_kernel, groups, owners), out_shape=...]
where the time goes in v6:
time: 71.8 us; the launch traced here: 71.6 us
  Pallas kernels  65.9 us (92%)
  local copies, waits for them, and re-layouts  4.42 us (6%)
  between operations  1.3 us (2%)
    pallas_call x1, Pallas kernels, on_device_kernel(): pl.pallas_call(functools.partial(step_kernel, groups, owners), out_shape=...  65.9 us
    unnamed x9, local copies, waits for them, and re-layouts  4.42 us

profile of v6, /device:TPU:0, one launch (start us, length us, event | category | flops | bytes accessed | tf_op | source)
XLA Modules:
  0.0 71.6 jit_solution(15503193779006726835)
XLA Ops:
  1.3 0.0 copy-start
  1.3 0.7 copy-done
  2.0 0.0 copy-start.1
  2.0 0.7 copy-done.1
  2.6 0.0 copy-start.2
  2.6 0.7 copy-done.2
  3.3 65.9 %shard_map.85 = (f32[1,192]{1,0:T(1,128)S(1)}, f32[24,64,128]{2,1,0:T(8,128)S(1)}, f32[16,128,128]{2,1,0:T(8,128)S(1)}) custom-call(s32[1,1,16]{2,1,0:T(1,128)S(1)} %copy-done.2, s32[4,1,16]{2,1,0:T(1,128)S(1)} %copy-done, s32[1,1]{1,0:T(1,128)S(6)} %copy.12.count, s32[1,192]{1,0:T(1,128)S(1)} %bitcast.6, bf16[192,64,128]{2,1,0:T(8,128)(2,1)} %fields_in.1, ...), custom_call_target="tpu_custom_call" | custom-call | flops 4000000000 | bytes 8000000 | tf_op jit(solution)/shard_map/pallas_call | solution.py:716
  69.2 0.6 copy.13
  69.7 0.9 %copy.14 = f32[24,64,128]{2,1,0:T(8,128)} copy(f32[24,64,128]{2,1,0:T(8,128)S(1)} %get-tuple-element.13) | data formatting | bytes 1572864
  70.6 1.0 %copy.15 = f32[1,1,16,128,128]{4,3,2,1,0:T(8,128)} copy(f32[1,1,16,128,128]{4,3,2,1,0:T(8,128)S(1)} %bitcast.4) | data formatting | bytes 2097152
Async XLA Ops:
  1.3 0.7 copy-start
  2.0 0.7 copy-start.1
  2.6 0.7 copy-start.2

commit v7 on v6

--- a/solution.py
+++ b/solution.py
@@ -275,7 +275,7 @@
         unit_m[pl.ds(t, 1), :] = big * (1.0 / TOP)
         return 0
 
-    lax.fori_loop(0, slots // 4, code_mats, 0, unroll=2)
+    lax.fori_loop(0, slots // 4, code_mats, 0, unroll=4)
     part = slots // 4
     mat_copies = [to_mate(send_m.at[pl.ds(h * part, part)], got_m.at[pl.ds(h * part, part)], sem_mat, h) for h in range(2)]
     mat_copies.append(to_mate(unit_m, got_unit_m, sem_mat, 2))
@@ -292,7 +292,7 @@
 
         lax.fori_loop(0, slots, turn, 0, unroll=4)
 
-    lax.fori_loop(slots // 4, slots // 2, code_mats, 0, unroll=2)
+    lax.fori_loop(slots // 4, slots // 2, code_mats, 0, unroll=4)
     turn_all(first_vec, first_t)
     total[...] = jnp.zeros_like(total)
 
@@ -486,7 +486,7 @@
             (msg3 if m else msg2)[w, pl.ds(q, 1), :] = big * (1.0 / TOP)
             return 0
 
-        lax.fori_loop(0, wing, code, 0)
+        lax.fori_loop(0, wing, code, 0, unroll=True)
 
     def partner(k):
         w, bit = o, 1
@@ -588,7 +588,7 @@
             mats_out[n * cap + c] = news[c]
         return 0
 
-    lax.fori_loop(0, slots // cap, last_update, 0)
+    lax.fori_loop(0, slots // cap, last_update, 0, unroll=2)
 
     col = err_col[pl.ds(pl.multiple_of(o * chunk, SUB), chunk), :]
     parts = chunk // SUB
@@ -663,7 +663,7 @@
         acc[...] += dot32(pick, jnp.concatenate(rows_of(terms_a) + rows_of(terms_b), axis=0))
         return 0
 
-    lax.fori_loop(0, groups * (owners // span), arrivals, 0)
+    lax.fori_loop(0, groups * (owners // span), arrivals, 0, unroll=2)
     for i in range(parts):
         grad_out[i * SUB : (i + 1) * SUB] = acc[:, i * feature : (i + 1) * feature].reshape(SUB, per_block, feature)
 

time: 71.8 us -> 71 us (0.989)
  Pallas kernels: 65.9 us -> 65.1 us
    pallas_call x1, Pallas kernels: 65.9 us -> 65.1 us  [on_device_kernel(): pl.pallas_call(functools.partial(step_kernel, groups, owners), out_shape=...]
where the time goes in v7:
time: 71 us; the launch traced here: 70.8 us
  Pallas kernels  65.1 us (92%)
  local copies, waits for them, and re-layouts  4.42 us (6%)
  between operations  1.3 us (2%)
    pallas_call x1, Pallas kernels, on_device_kernel(): pl.pallas_call(functools.partial(step_kernel, groups, owners), out_shape=...  65.1 us
    unnamed x9, local copies, waits for them, and re-layouts  4.42 us

profile of v7, /device:TPU:0, one launch (start us, length us, event | category | flops | bytes accessed | tf_op | source)
XLA Modules:
  0.0 70.8 jit_solution(14836179861987552164)
XLA Ops:
  1.3 0.0 copy-start
  1.3 0.7 copy-done
  2.0 0.0 copy-start.1
  2.0 0.7 copy-done.1
  2.6 0.0 copy-start.2
  2.6 0.7 copy-done.2
  3.3 65.1 %shard_map.85 = (f32[1,192]{1,0:T(1,128)S(1)}, f32[24,64,128]{2,1,0:T(8,128)S(1)}, f32[16,128,128]{2,1,0:T(8,128)S(1)}) custom-call(s32[1,1,16]{2,1,0:T(1,128)S(1)} %copy-done.2, s32[4,1,16]{2,1,0:T(1,128)S(1)} %copy-done, s32[1,1]{1,0:T(1,128)S(6)} %copy.12.count, s32[1,192]{1,0:T(1,128)S(1)} %bitcast.6, bf16[192,64,128]{2,1,0:T(8,128)(2,1)} %fields_in.1, ...), custom_call_target="tpu_custom_call" | custom-call | flops 4000000000 | bytes 8000000 | tf_op jit(solution)/shard_map/pallas_call | solution.py:716
  68.4 0.6 copy.13
  68.9 0.9 %copy.14 = f32[24,64,128]{2,1,0:T(8,128)} copy(f32[24,64,128]{2,1,0:T(8,128)S(1)} %get-tuple-element.13) | data formatting | bytes 1572864
  69.8 1.0 %copy.15 = f32[1,1,16,128,128]{4,3,2,1,0:T(8,128)} copy(f32[1,1,16,128,128]{4,3,2,1,0:T(8,128)S(1)} %bitcast.4) | data formatting | bytes 2097152
Async XLA Ops:
  1.3 0.7 copy-start
  2.0 0.7 copy-start.1
  2.6 0.7 copy-start.2
